TPU v7x, 32 devices: a whole 2x2x4 slice. The times are simulated.
32 devices in a mesh: row: 4 (over y, x), col: 8 (over z, core).
Axes of the slice: x: 2, y: 2, z: 4, core: 2. Of those that a mesh axis runs over, the one named last changes fastest.
Arguments:
- stream_in: bfloat16 [1024, 8192], P('col', 'row'), may hold values from -6 to 6
- grad_out: bfloat16 [1024, 8192], P('col', 'row'), may hold values from -6 to 6
- gate_pre: bfloat16 [1024, 14336], P('row', 'col'), may hold values from -6 to 6
- up_pre: bfloat16 [1024, 14336], P('row', 'col'), may hold values from -6 to 6
- keep_mask: int32 [1024, 14336], P('row', 'col'), may hold values 0 or 1
- segment_ids: int32 [1024], P('row'), may hold values from 0 to 15, never falling along the last dimension, each value on 1 to 128 neighbouring positions
- norm_gain: float32 [8192], P('row'), may hold values from 0.25 to 1.75
- w_gate: bfloat16 [8192, 14336], P('row', 'col'), may hold values from -0.0625 to 0.0625
- w_up: bfloat16 [8192, 14336], P('row', 'col'), may hold values from -0.0625 to 0.0625
- w_down: bfloat16 [14336, 8192], P('col', 'row'), may hold values from -0.046875 to 0.046875
Outputs:
- grad_in: bfloat16 [1024, 8192], P('col', 'row')
- grad_gate: bfloat16 [8192, 14336], P('row', 'col')
- grad_up: bfloat16 [8192, 14336], P('row', 'col')
- grad_down: bfloat16 [14336, 8192], P('col', 'row')
Inputs may be any that keep to these rules, and one draw needn't show every extreme that they name: `segment_ids`: never falls along the tokens; each of the 16 documents has 1 to 128 tokens, one exactly 128.
All inputs are finite; a program needn't handle non-finite values. No bound on the sum of `keep_mask` on one device may be relied on, other than what follows from the above.
Results may differ from a plain program's by a relative error of at most 0.0059.
Values may be sent and summed in bfloat16 or wider, within the bound.
No kernel may reach another device: no remote copies, remote signals or barrier semaphores. Data moves between devices by JAX's collectives and lax.ppermute only.
A program may use at most 128 MiB of HBM per device.

v0:
```python
import jax
import jax.numpy as jnp
from jax import lax
from jax.sharding import PartitionSpec as P

D = 8192
SEGS = 16


eps = 1e-05
keep_scale = 1.0 / 0.9


def over_tokens(left, right):
    return lax.dot_general(
        left, right, (((0,), (0,)), ((), ())), preferred_element_type=jnp.float32
    )


def over_width(left, right):
    return lax.dot_general(
        left, right, (((1,), (1,)), ((), ())), preferred_element_type=jnp.float32
    )


def per_device(
    stream_in, grad_out, gate_pre, up_pre, keep_mask, segment_ids, norm_gain, w_gate, w_up, w_down
):
    n_row = lax.axis_size("row")
    n_col = lax.axis_size("col")
    tok_col, feat_loc = stream_in.shape
    total = tok_col * n_col
    xs = stream_in.astype(jnp.float32)
    onehot = (segment_ids[:, None] == jnp.arange(SEGS, dtype=jnp.int32)[None, :]).astype(
        jnp.float32
    )
    squares, counts = lax.psum((jnp.sum(xs * xs, axis=1), jnp.sum(onehot, axis=0)), "row")
    weights = jnp.sum(onehot * (total / (SEGS * counts))[None, :], axis=1)
    recip = lax.rsqrt(squares / D + eps)
    normed = (xs * recip[:, None] * norm_gain[None, :]).astype(jnp.bfloat16)
    gate_f = gate_pre.astype(jnp.float32)
    up_f = up_pre.astype(jnp.float32)
    sig = jax.nn.sigmoid(gate_f)
    keep_f = keep_mask.astype(jnp.float32) * keep_scale
    dropped = (gate_f * sig * up_f * keep_f * weights[:, None]).astype(jnp.bfloat16)
    cot_full, normed_full = (
        lax.all_gather(grad_out, "col", axis=0, tiled=True),
        lax.all_gather(normed, "col", axis=0, tiled=True),
    )
    back = lax.psum_scatter(over_width(cot_full, w_down), "row", scatter_dimension=0, tiled=True)
    grad_act = back * weights[:, None] * keep_f
    grad_gpre = (grad_act * up_f * sig * (1.0 + gate_f * (1.0 - sig))).astype(jnp.bfloat16)
    grad_upre = (grad_act * gate_f * sig).astype(jnp.bfloat16)
    dropped_full, gpre_full, upre_full = (
        lax.all_gather(dropped, "row", axis=0, tiled=True),
        lax.all_gather(grad_gpre, "row", axis=0, tiled=True),
        lax.all_gather(grad_upre, "row", axis=0, tiled=True),
    )
    grad_down = over_tokens(dropped_full, cot_full).astype(jnp.bfloat16)
    grad_gate = over_tokens(normed_full, gpre_full).astype(jnp.bfloat16)
    grad_up = over_tokens(normed_full, upre_full).astype(jnp.bfloat16)
    grad_normed = lax.psum_scatter(
        over_width(gpre_full, w_gate) + over_width(upre_full, w_up),
        "col",
        scatter_dimension=0,
        tiled=True,
    )
    scaled = grad_normed * norm_gain[None, :]
    per_dev = tok_col // n_row
    x_rows = lax.all_to_all(
        xs.reshape(n_row, per_dev, feat_loc), "row", split_axis=0, concat_axis=2, tiled=True
    )
    d_rows = lax.all_to_all(
        scaled.reshape(n_row, per_dev, feat_loc), "row", split_axis=0, concat_axis=2, tiled=True
    )
    row_recip = lax.rsqrt(jnp.mean(x_rows * x_rows, axis=2, keepdims=True) + eps)
    row_inner = jnp.mean(d_rows * x_rows, axis=2, keepdims=True)
    result = row_recip * (d_rows - x_rows * row_recip * row_recip * row_inner)
    moved = lax.all_to_all(result, "row", split_axis=2, concat_axis=0, tiled=True)
    branch = moved.reshape(tok_col, feat_loc)
    grad_in = (grad_out.astype(jnp.float32) + branch).astype(jnp.bfloat16)
    return (grad_in, grad_gate, grad_up, grad_down)


def solution(mesh):
    return jax.shard_map(
        per_device,
        mesh=mesh,
        in_specs=(
            P("col", "row"),
            P("col", "row"),
            P("row", "col"),
            P("row", "col"),
            P("row", "col"),
            P("row"),
            P("row"),
            P("row", "col"),
            P("row", "col"),
            P("col", "row"),
        ),
        out_specs=(P("col", "row"), P("row", "col"), P("row", "col"), P("col", "row")),
        check_vma=False,
    )
```

profile of v0, /device:TPU:0, one launch (start us, length us, event | category | flops | bytes accessed | tf_op | source)
XLA Modules:
  0.0 526.7 jit_solution(1315302157284409897)
XLA Ops:
  7.2 0.7 all-gather.6.cloned.1.call-update
  7.9 51.5 %all-gather.6.cloned.1.call-done = bf16[1024,2048]{1,0:T(8,128)(2,1)} async-done(((bf16[128,2048]{1,0:T(8,128)(2,1)}), bf16[1024,2048]{1,0:T(8,128)(2,1)}) %all-gather.6.cloned.1.call-update) | async-done | bytes 4194320 | tf_op jit(solution)/shard_map/all_gather | solution.py:47
  59.5 13.6 %fusion.15 = f32[1024,1792]{1,0:T(8,128)} fusion(bf16[1024,2048]{1,0:T(8,128)(2,1)} %all-gather.6.cloned.1.call-done, bf16[1792,2048]{1,0:T(8,128)(2,1)} %param.19), kind=kOutput, calls=%fused_computation.41 | convolution fusion | flops 7516192768 | bytes 18874368 | tf_op jit(solution)/shard_map/dot_general | solution.py:21
  73.1 0.9 copy-done
  74.4 10.0 %all-reduce = (f32[16]{0:T(128)S(1)}, f32[128]{0:T(128)S(1)}) all-reduce(f32[16]{0:T(128)S(1)} %convert_reduce_fusion, f32[128]{0:T(128)S(1)} %multiply_reduce_fusion), channel_id=1, replica_groups=mesh['row'=4,'col'=8] {'row'}, use_global_device_ids=true, to_apply=%region_3.0 | all-reduce | flops 144 | bytes 1152 | tf_op jit(solution)/shard_map/psum | solution.py:37
  84.5 66.4 %reduce-scatter.3.cloned.1.call-done = f32[256,1792]{1,0:T(8,128)} async-done(((f32[1024,1792]{1,0:T(8,128)}), f32[256,1792]{1,0:T(8,128)}) %reduce-scatter.3.cloned.1.call-update) | async-done | bytes 1835024 | tf_op jit(solution)/shard_map/reduce_scatter | solution.py:50
  151.0 4.7 fusion.11
  155.8 0.5 all-gather.10.cloned.1.call-update
  156.4 47.8 %all-gather.8.cloned.1.call-done = bf16[1024,1792]{1,0:T(8,128)(2,1)} async-done(((bf16[256,1792]{1,0:T(8,128)(2,1)}), bf16[1024,1792]{1,0:T(8,128)(2,1)}) %all-gather.8.cloned.1.call-update) | async-done | bytes 3670032 | tf_op jit(solution)/shard_map/all_gather | solution.py:56
  204.2 13.2 %fusion.16 = f32[1024,2048]{1,0:T(8,128)} fusion(bf16[1024,1792]{1,0:T(8,128)(2,1)} %all-gather.8.cloned.1.call-done, bf16[2048,1792]{1,0:T(8,128)(2,1)} %param.17), kind=kOutput, calls=%fused_computation.42 | convolution fusion | flops 7516192768 | bytes 19398656 | tf_op jit(solution)/shard_map/dot_general | solution.py:21
  217.4 37.5 %all-gather.10.cloned.1.call-done = bf16[1024,1792]{1,0:T(8,128)(2,1)} async-done(((bf16[256,1792]{1,0:T(8,128)(2,1)}), bf16[1024,1792]{1,0:T(8,128)(2,1)}) %all-gather.10.cloned.1.call-update) | async-done | bytes 3670032 | tf_op jit(solution)/shard_map/all_gather | solution.py:57
  254.9 14.4 %convolution_add_fusion = f32[1024,2048]{1,0:T(8,128)} fusion(f32[1024,2048]{1,0:T(8,128)} %fusion.16, bf16[1024,1792]{1,0:T(8,128)(2,1)} %all-gather.10.cloned.1.call-done, bf16[2048,1792]{1,0:T(8,128)(2,1)} %param.18), kind=kOutput, calls=%fused_computation.3 | convolution fusion | flops 7518289920 | bytes 27787264 | tf_op jit(solution)/shard_map/dot_general | solution.py:21
  269.3 0.5 all-gather.14.cloned.1.call-update
  269.9 89.1 %reduce-scatter.5.cloned.1.call-done = f32[128,2048]{1,0:T(8,128)} async-done(((f32[1024,2048]{1,0:T(8,128)}), f32[128,2048]{1,0:T(8,128)}) %reduce-scatter.5.cloned.1.call-update) | async-done | bytes 1048592 | tf_op jit(solution)/shard_map/reduce_scatter | solution.py:62
  359.1 2.6 multiply_convert_fusion
  361.7 26.4 %all_to_all.51 = f32[4,32,2048]{2,1,0:T(8,128)S(1)} all-to-all(f32[4,32,2048]{2,1,0:T(8,128)S(1)} %convert), channel_id=1, replica_groups=mesh['row'=4,'col'=8] {'row'}, dimensions={0} | all-to-all | bytes 2097152 | tf_op jit(solution)/shard_map/all_to_all | solution.py:70
  388.1 3.7 all-to-all-start.1
  391.9 20.2 %all-to-all-done.1 = f32[4,32,2048]{2,1,0:T(8,128)S(1)} async-done(((f32[4,32,2048]{2,1,0:T(8,128)}), f32[4,32,2048]{2,1,0:T(8,128)S(1)}, u32[]{:S(2)}, u32[]{:S(2)}) %all-to-all-start.1) | async-done | bytes 1048608 | tf_op jit(solution)/shard_map/all_to_all | solution.py:73
  412.2 0.3 fusion.14
  412.8 6.5 %copy.26 = f32[1,32,8192]{1,0,2:T(1,128)} copy(f32[1,32,8192]{2,1,0:T(8,128)S(1)} %subtract_multiply_fusion) | data formatting | bytes 2097152 | tf_op jit(solution)/shard_map/mul | solution.py:78
  419.3 0.5 broadcast.117
  419.8 38.5 %reduce.4 = f32[8192,32]{1,0:T(8,128)} reduce(f32[8192,1,32]{2,1,0:T(1,128)} %bitcast.41, f32[]{:T(128)} %broadcast.117), dimensions={1}, to_apply=%bitcast.26.reduce_sub_computation | reduce | bytes 2097156
  458.3 4.9 reshape.168
  463.1 3.5 all-to-all-start.2
  466.7 12.8 %convolution_convert_fusion = bf16[1792,2048]{1,0:T(8,128)(2,1)} fusion(bf16[1024,1792]{1,0:T(8,128)(2,1)} %all-gather.14.cloned.1.call-done, bf16[1024,2048]{1,0:T(8,128)(2,1)} %all-gather.6.cloned.1.call-done), kind=kOutput, calls=%fused_computation | convolution fusion | flops 7519862784 | bytes 15204352 | tf_op jit(solution)/shard_map/dot_general | solution.py:15
  479.5 3.7 reduce.5
  483.2 8.2 %reshape.169 = f32[8192,1,32]{2,1,0:T(1,128)} reshape(f32[4,65536]{1,0:T(4,128)S(1)} %reduce.5) | data formatting | bytes 2097152
  491.4 3.1 copy.29
  494.6 0.6 copy.28
  495.2 0.9 fusion.12
  496.1 13.0 %convolution_convert_fusion.1 = bf16[2048,1792]{1,0:T(8,128)(2,1)} fusion(bf16[1024,2048]{1,0:T(8,128)(2,1)} %all-gather.12.cloned.1.call-done, bf16[1024,1792]{1,0:T(8,128)(2,1)} %all-gather.10.cloned.1.call-done), kind=kOutput, calls=%fused_computation.1 | convolution fusion | flops 7519862784 | bytes 15204352 | tf_op jit(solution)/shard_map/dot_general | solution.py:15
  509.1 10.3 %convolution_convert_fusion.2 = bf16[2048,1792]{1,0:T(8,128)(2,1)} fusion(bf16[1024,2048]{1,0:T(8,128)(2,1)S(1)} %copy-done.6, bf16[1024,1792]{1,0:T(8,128)(2,1)S(1)} %copy-done.7), kind=kOutput, calls=%fused_computation.2 | convolution fusion | flops 7519862784 | bytes 15204352 | tf_op jit(solution)/shard_map/dot_general | solution.py:15
  (39 shorter events, 1.3 us)
Async XLA Ops:
  7.2 52.3 %all-gather.6.cloned.1.call-start = ((), (), s32[]{:S(2)}) async-start(), calls=%async_computation.5 | async-start | bytes 4718592 | tf_op jit(solution)/shard_map/all_gather | solution.py:47
  7.9 143.1 %reduce-scatter.3.cloned.1.call-start = ((), (), s32[]{:S(2)}) async-start(), calls=%async_computation.6 | async-start | bytes 9175040 | tf_op jit(solution)/shard_map/reduce_scatter | solution.py:50
  73.0 1.0 copy-start
  73.0 1.2 copy-start.5
  73.0 77.9 %copy-start.2 = (s32[256,1792]{1,0:T(8,128)S(1)}, s32[256,1792]{1,0:T(8,128)}, u32[]{:S(2)}) copy-start(s32[256,1792]{1,0:T(8,128)} %param.14) | copy-start | bytes 5505028
  73.1 77.9 %copy-start.3 = (bf16[256,1792]{1,0:T(8,128)(2,1)S(1)}, bf16[256,1792]{1,0:T(8,128)(2,1)}, u32[]{:S(2)}) copy-start(bf16[256,1792]{1,0:T(8,128)(2,1)} %param.12) | copy-start | bytes 2752516
  73.1 131.1 %all-gather.8.cloned.1.call-start = ((), (), s32[]{:S(2)}) async-start(), calls=%async_computation.7 | async-start | bytes 4587520 | tf_op jit(solution)/shard_map/all_gather | solution.py:56
  155.7 99.1 %all-gather.10.cloned.1.call-start = ((), (), s32[]{:S(2)}) async-start(), calls=%async_computation.8 | async-start | bytes 4587520 | tf_op jit(solution)/shard_map/all_gather | solution.py:57
  156.3 202.7 %reduce-scatter.5.cloned.1.call-start = ((), (), s32[]{:S(2)}) async-start(), calls=%async_computation.9 | async-start | bytes 9437184 | tf_op jit(solution)/shard_map/reduce_scatter | solution.py:62
  269.3 89.8 %copy-start.4 = (f32[2048]{0:T(1024)S(1)}, f32[2048]{0:T(1024)}, u32[]{:S(2)}) copy-start(f32[2048]{0:T(1024)} %param.16) | copy-start | bytes 24580
  269.3 197.4 %all-gather.14.cloned.1.call-start = ((), (), s32[]{:S(2)}) async-start(), calls=%async_computation.11 | async-start | bytes 4587520 | tf_op jit(solution)/shard_map/all_gather | solution.py:55
  269.9 226.2 %all-gather.12.cloned.1.call-start = ((), (), s32[]{:S(2)}) async-start(), calls=%async_computation.10 | async-start | bytes 4718592 | tf_op jit(solution)/shard_map/all_gather | solution.py:48
  388.1 24.0 %all-to-all-start.1 = ((f32[4,32,2048]{2,1,0:T(8,128)}), f32[4,32,2048]{2,1,0:T(8,128)S(1)}, u32[]{:S(2)}, u32[]{:S(2)}) async-start(f32[4,32,2048]{2,1,0:T(8,128)} %bitcast.3), calls=%async_computation.3 | async-start | bytes 2097152 | tf_op jit(solution)/shard_map/all_to_all | solution.py:73
  463.1 16.4 %all-to-all-start.2 = ((f32[4,1,65536]{2,1,0:T(1,128)}), f32[4,1,65536]{2,1,0:T(1,128)S(1)}, u32[]{:S(2)}, u32[]{:S(2)}) async-start(f32[4,1,65536]{2,1,0:T(1,128)} %reshape.168), calls=%async_computation.4 | async-start | bytes 2097152 | tf_op jit(solution)/shard_map/all_to_all | solution.py:79
  491.4 3.7 copy-start.1
  496.1 13.0 %copy-start.6 = (bf16[1024,2048]{1,0:T(8,128)(2,1)S(1)}, bf16[1024,2048]{1,0:T(8,128)(2,1)}, u32[]{:S(2)}) copy-start(bf16[1024,2048]{1,0:T(8,128)(2,1)} %all-gather.12.cloned.1.call-done) | copy-start | bytes 12582916
  496.1 13.0 %copy-start.7 = (bf16[1024,1792]{1,0:T(8,128)(2,1)S(1)}, bf16[1024,1792]{1,0:T(8,128)(2,1)}, u32[]{:S(2)}) copy-start(bf16[1024,1792]{1,0:T(8,128)(2,1)} %all-gather.8.cloned.1.call-done) | copy-start | bytes 11010052
Sparse Core Ops, SparseCore 0:
  9.6 49.8 all-gather.5
  73.2 77.7 reduce-scatter.2
  155.9 48.3 all-gather.7
  206.5 48.3 all-gather.9
  269.4 89.5 reduce-scatter.4
  360.8 59.0 all-gather.13
  421.4 48.3 all-gather.11
where the time goes:
time: 535 us; the launch traced here: 527 us
  waiting for transfers between devices  314 us (59%)
  matrix products  77.3 us (14%)
  other arithmetic  51.4 us (10%)
  blocking collectives  36.4 us (7%)
  local copies, waits for them, and re-layouts  24.9 us (5%)
  between operations  14.7 us (3%)
  starting transfers between devices  7.49 us (1%)
    reduce_scatter x1, waiting for transfers between devices, per_device(): lax.psum_scatter(over_width(gpre_full, w_gate) + over_width(upre_full, w_...  89.1 us
    reduce_scatter x1, waiting for transfers between devices, per_device(): lax.psum_scatter(over_width(cot_full, w_down), 'row', scatter_dimension=0...  66.4 us
    all_gather x1, waiting for transfers between devices, per_device(): lax.all_gather(grad_out, 'col', axis=0, tiled=True)  51.5 us
    all_gather x1, waiting for transfers between devices, per_device(): lax.all_gather(grad_gpre, 'row', axis=0, tiled=True)  47.8 us
    dot_general x3, matrix products, over_width(): lax.dot_general(left, right, (((1,), (1,)), ((), ())), preferred_element_...  41.2 us
    unnamed x1, other arithmetic  38.5 us
    all_gather x1, waiting for transfers between devices, per_device(): lax.all_gather(grad_upre, 'row', axis=0, tiled=True)  37.5 us
    dot_general x3, matrix products, over_tokens(): lax.dot_general(left, right, (((0,), (0,)), ((), ())), preferred_element_...  36.2 us
  transfers between devices with their start and end apart: 9, of which 6 were waited for; matrix products, arithmetic and copies ran while one was open for 18% of the time, Pallas kernels for 0%

commit v1 on v0

v1 whole, which is shorter than its diff:
```python
import functools

import jax
import jax.numpy as jnp
from jax import lax
from jax.experimental import pallas as pl
from jax.experimental.pallas import tpu as pltpu
from jax.sharding import PartitionSpec as P

D = 8192
SEGS = 16
CHUNKS = 2

eps = 1e-05
keep_scale = 1.0 / 0.9
bf16 = jnp.bfloat16
f32 = jnp.float32
ANY = pl.BlockSpec(memory_space=pl.ANY)


def over_tokens(left, right):
    return lax.dot_general(left, right, (((0,), (0,)), ((), ())), preferred_element_type=f32)


def over_width(left, right):
    return lax.dot_general(left, right, (((1,), (1,)), ((), ())), preferred_element_type=f32)


def join_kernel(n, *refs):
    parts, out, sems = refs[:n], refs[-2], refs[-1]
    copies = [pltpu.make_async_copy(parts[s], out.at[s], sems.at[s]) for s in range(n)]
    for copy in copies:
        copy.start()
    for copy in copies:
        copy.wait()


def join(parts, after=()):
    n = len(parts)
    shape = (n,) + parts[0].shape
    return pl.pallas_call(
        functools.partial(join_kernel, n),
        out_shape=jax.ShapeDtypeStruct(shape, parts[0].dtype),
        in_specs=[ANY] * (n + len(after)),
        scratch_shapes=[pltpu.SemaphoreType.DMA((n,))],
        compiler_params=pltpu.CompilerParams(vmem_limit_bytes=32 * 1024 * 1024),
        cost_estimate=pl.CostEstimate(
            flops=0, bytes_accessed=4 * n * parts[0].size, transcendentals=0
        ),
    )(*parts, *after)


def fill(n, where, mine, other, out, sems):
    core = where[0]
    copies = []
    for s in range(n):
        copies.append(pltpu.make_async_copy(mine.at[s], out.at[where[1 + s], core], sems.at[s]))
        copies.append(
            pltpu.make_async_copy(other.at[s], out.at[where[1 + s], 1 - core], sems.at[n + s])
        )
    for copy in copies:
        copy.start()
    for copy in copies:
        copy.wait()


def place_kernel(n, where, mine, other, *refs):
    fill(n, where, mine, other, refs[-2], refs[-1])


def place(where, mine, other, after=()):
    n, shape = mine.shape[0], mine.shape[1:]
    return pl.pallas_call(
        functools.partial(place_kernel, n),
        out_shape=jax.ShapeDtypeStruct((n, 2) + shape, mine.dtype),
        in_specs=[pl.BlockSpec(memory_space=pltpu.SMEM)] + [ANY] * (2 + len(after)),
        scratch_shapes=[pltpu.SemaphoreType.DMA((2 * n,))],
        compiler_params=pltpu.CompilerParams(vmem_limit_bytes=32 * 1024 * 1024),
        cost_estimate=pl.CostEstimate(flops=0, bytes_accessed=8 * mine.size, transcendentals=0),
    )(where, mine, other, *after)


def back_kernel(n, where, mine, other, w_ref, *refs):
    cot, part, sems = refs[-3:]

    @pl.when(pl.program_id(0) == 0)
    def _():
        fill(n, where, mine, other, cot, sems)

    left = cot[...].reshape(-1, cot.shape[-1])
    out = over_width(left, w_ref[...]).astype(bf16)
    part[...] = out.reshape(part.shape)


def back(where, mine, other, w_down, after=()):
    n, sub, feat = mine.shape
    width = w_down.shape[0]
    tile = width // 2 if width // 2 % 128 == 0 else width
    tokens = 2 * n * sub
    return pl.pallas_call(
        functools.partial(back_kernel, n),
        out_shape=(
            jax.ShapeDtypeStruct((n, 2, sub, feat), bf16),
            jax.ShapeDtypeStruct((n, 2 * sub, width), bf16),
        ),
        grid=(width // tile,),
        in_specs=[
            pl.BlockSpec(memory_space=pltpu.SMEM),
            ANY,
            ANY,
            pl.BlockSpec((tile, feat), lambda i: (i, 0)),
        ]
        + [ANY] * len(after),
        out_specs=(
            pl.BlockSpec((n, 2, sub, feat), lambda i: (0, 0, 0, 0)),
            pl.BlockSpec((n, 2 * sub, tile), lambda i: (0, 0, i)),
        ),
        scratch_shapes=[pltpu.SemaphoreType.DMA((2 * n,))],
        compiler_params=pltpu.CompilerParams(vmem_limit_bytes=48 * 1024 * 1024),
        cost_estimate=pl.CostEstimate(
            flops=2 * tokens * width * feat,
            bytes_accessed=2 * (2 * tokens * feat + width * feat + tokens * width),
            transcendentals=0,
        ),
    )(where, mine, other, w_down, *after)


def dropped_kernel(gate_ref, up_ref, keep_ref, weight_ref, *refs):
    out = refs[-1]
    for k in range(CHUNKS):
        gate = gate_ref[:, k].astype(f32)
        scale = keep_ref[:, k].astype(f32) * keep_scale * weight_ref[:, k]
        value = gate * jax.nn.sigmoid(gate) * up_ref[:, k].astype(f32) * scale
        out[k] = value.astype(bf16).reshape(out.shape[1:])


def masked(gate, up, keep, weights):
    two, chunks, sub, width = gate.shape
    tile = 256 if width % 256 == 0 else 128
    block = pl.BlockSpec((two, chunks, sub, tile), lambda i: (0, 0, 0, i))
    return pl.pallas_call(
        dropped_kernel,
        out_shape=jax.ShapeDtypeStruct((chunks, two * sub, width), bf16),
        grid=(width // tile,),
        in_specs=[
            block,
            block,
            block,
            pl.BlockSpec((two, chunks, sub, 1), lambda i: (0, 0, 0, 0)),
        ],
        out_specs=pl.BlockSpec((chunks, two * sub, tile), lambda i: (0, 0, i)),
        cost_estimate=pl.CostEstimate(
            flops=10 * gate.size, bytes_accessed=10 * gate.size, transcendentals=gate.size
        ),
    )(gate, up, keep, weights)


def grads_kernel(n, *refs):
    own, parts = refs[0], refs[1:n]
    gate_ref, up_ref, keep_ref, weight_ref = refs[n : n + 4]
    out = refs[-1]
    total = own[0].astype(f32)
    for part in parts:
        total = total + part[...].astype(f32)
    two, sub, tile = gate_ref.shape
    total = total.reshape(two, sub, tile)
    gate, up = gate_ref[...].astype(f32), up_ref[...].astype(f32)
    act = total * (keep_ref[...].astype(f32) * keep_scale * weight_ref[...])
    sig = jax.nn.sigmoid(gate)
    out[0] = (act * up * sig * (1.0 + gate * (1.0 - sig))).astype(bf16).reshape(out.shape[1:])
    out[1] = (act * gate * sig).astype(bf16).reshape(out.shape[1:])


def hidden_grads(k, own, parts, gate, up, keep, weights, after=()):
    n = 1 + len(parts)
    two, chunks, sub, width = gate.shape
    tile = 256 if width % 256 == 0 else 128
    block = pl.BlockSpec((two, None, sub, tile), lambda i: (0, k, 0, i))
    size = two * sub * width
    return pl.pallas_call(
        functools.partial(grads_kernel, n),
        out_shape=jax.ShapeDtypeStruct((2, two * sub, width), bf16),
        grid=(width // tile,),
        in_specs=[pl.BlockSpec((1, two * sub, tile), lambda i: (0, 0, i))]
        + [pl.BlockSpec((two * sub, tile), lambda i: (0, i))] * (n - 1)
        + [block] * 3
        + [pl.BlockSpec((two, None, sub, 1), lambda i: (0, k, 0, 0))]
        + [ANY] * len(after),
        out_specs=pl.BlockSpec((2, two * sub, tile), lambda i: (0, 0, i)),
        cost_estimate=pl.CostEstimate(
            flops=20 * size, bytes_accessed=(12 + 2 * n) * size, transcendentals=size
        ),
    )(own, *parts, gate, up, keep, weights, *after)


def hidden_kernel(n, where_ref, gpre_ref, upre_ref, wg_ref, wu_ref, *refs):
    give_ref, keep_ref = refs[-2:]
    core = where_ref[0]
    shift = where_ref[1]
    part = over_width(gpre_ref[...], wg_ref[...]) + over_width(upre_ref[...], wu_ref[...])
    sub = give_ref.shape[1]
    part = part.reshape(n, 2, sub, part.shape[1])
    low = core == 0
    for j in range(n):
        at = lax.bitwise_xor(shift, j)
        keep_ref[at] = jnp.where(low, part[j, 0], part[j, 1])
        give_ref[at] = jnp.where(low, part[j, 1], part[j, 0]).astype(bf16)


def hidden(where, gpre, upre, w_gate, w_up, n, after=()):
    tokens, width = gpre.shape
    feat = w_gate.shape[0]
    tile = min(512, feat)
    sub = tokens // (2 * n)
    return pl.pallas_call(
        functools.partial(hidden_kernel, n),
        out_shape=(
            jax.ShapeDtypeStruct((n, sub, feat), bf16),
            jax.ShapeDtypeStruct((n, sub, feat), f32),
        ),
        grid_spec=pltpu.PrefetchScalarGridSpec(
            num_scalar_prefetch=1,
            grid=(feat // tile,),
            in_specs=[
                pl.BlockSpec((tokens, width), lambda i, w: (0, 0)),
                pl.BlockSpec((tokens, width), lambda i, w: (0, 0)),
                pl.BlockSpec((tile, width), lambda i, w: (i, 0)),
                pl.BlockSpec((tile, width), lambda i, w: (i, 0)),
            ]
            + [ANY] * len(after),
            out_specs=(
                pl.BlockSpec((n, sub, tile), lambda i, w: (0, 0, i)),
                pl.BlockSpec((n, sub, tile), lambda i, w: (0, 0, i)),
            ),
        ),
        compiler_params=pltpu.CompilerParams(vmem_limit_bytes=48 * 1024 * 1024),
        cost_estimate=pl.CostEstimate(
            flops=4 * tokens * width * feat,
            bytes_accessed=4 * width * (tokens + feat) + 6 * n * sub * feat,
            transcendentals=0,
        ),
    )(where, gpre, upre, w_gate, w_up, *after)


def per_device(
    stream_in, grad_out, gate_pre, up_pre, keep_mask, segment_ids, norm_gain, w_gate, w_up, w_down
):
    n_row = lax.axis_size("row")
    n_col = lax.axis_size("col")
    nz = n_col // 2
    tok_col, feat = stream_in.shape
    tok_row, width = gate_pre.shape
    total = tok_col * n_col
    sub = tok_col // CHUNKS
    col, row = lax.axis_index("col"), lax.axis_index("row")
    core, chip = lax.rem(col, 2), lax.div(col, 2)
    ring = [0] + list(range(1, nz, 2)) + list(range(nz - 2 + nz % 2, 0, -2))
    after_of = {ring[i]: ring[(i + 1) % nz] for i in range(nz)}

    def spots(chips):
        return jnp.stack([core] + [lax.bitwise_xor(c, row) for c in chips]).astype(jnp.int32)

    direct = spots([lax.bitwise_xor(chip, s) for s in range(nz)])
    held = [sum(jnp.where(chip == ring[p], ring[(p - s) % nz], 0) for p in range(nz)) for s in range(nz)]
    around = spots(held)

    def swap(a):
        return lax.ppermute(a, "col", [(i, i ^ 1) for i in range(n_col)])

    def z_step(a, s):
        return lax.ppermute(a, "col", [(i, i ^ (2 * s)) for i in range(n_col)])

    def z_next(a):
        return lax.ppermute(a, "col", [(i, 2 * after_of[i // 2] + i % 2) for i in range(n_col)])

    def row_step(a, j):
        return lax.ppermute(a, "row", [(i, i ^ j) for i in range(n_row)])

    def row_near(a):
        got = {0: a, 1: row_step(a, 1)}
        for k in range(2, n_row, 2):
            got[k] = row_step(a, k)
        return got

    def row_far(got):
        halves = {j: (got[j][0], got[j][1]) for j in got}
        for k in range(2, n_row, 2):
            halves[k + 1] = (row_step(got[1][0], k), row_step(got[k][1], 1))
        return [[halves[j][h] for j in range(n_row)] for h in range(2)]

    def row_total(a):
        got = a
        for j in range(1, n_row):
            got = got + row_step(a, j)
        return got

    def cot_part(k):
        a = grad_out[k * sub : (k + 1) * sub]
        mine = join([a] + [z_step(a, s) for s in range(1, nz)])
        return mine, swap(mine)

    xs = stream_in.astype(f32)
    onehot = (segment_ids[:, None] == jnp.arange(SEGS, dtype=jnp.int32)[None, :]).astype(f32)
    sums = row_total(jnp.concatenate([jnp.sum(xs * xs, axis=1), jnp.sum(onehot, axis=0)]))
    squares, counts = sums[:tok_col], sums[tok_col:]
    weights = jnp.sum(onehot * (total / (SEGS * counts))[None, :], axis=1)
    weights = weights.reshape(2, CHUNKS, sub, 1)
    recip = lax.rsqrt(squares / D + eps)
    normed = (xs * recip[:, None] * norm_gain[None, :]).astype(bf16)

    gate, up, keep = (a.reshape(2, CHUNKS, sub, width) for a in (gate_pre, up_pre, keep_mask))
    drop_near = row_near(masked(gate, up, keep, weights))

    cots, partials = [], []
    for k in range(CHUNKS):
        mine, other = cot_part(k)
        late = [drop_near[j] for j in drop_near if j] if k == CHUNKS - 1 else []
        cot, partial = back(direct, mine, other, w_down, late)
        cots.append(cot)
        partials.append(partial)
    drop_far = row_far(drop_near)
    dropped_full = jnp.concatenate([s for half in drop_far for s in half], axis=0)

    norm_slots = [normed]
    for s in range(1, nz):
        norm_slots.append(z_next(norm_slots[-1]))

    gathered = []
    for k in range(CHUNKS):
        parts = [row_step(partials[k][j], j) for j in range(1, n_row)]
        late = []
        if k == CHUNKS - 1:
            late = [drop_far[h][j] for h in range(2) for j in range(3, n_row, 2)] + [norm_slots[1]]
        near = row_near(hidden_grads(k, partials[k], parts, gate, up, keep, weights, late))
        gathered.append(near)

    cot_full = jnp.concatenate([c.reshape(-1, feat) for c in cots], axis=0)
    grad_down = over_tokens(dropped_full, cot_full).astype(bf16)

    normed_mine = join(norm_slots)
    normed_full = place(around, normed_mine, swap(normed_mine))
    gathered = [[jnp.concatenate(s, axis=0) for s in row_far(near)] for near in gathered]

    scaled = []
    for k in range(CHUNKS):
        late = [grad_down] + norm_slots[2:] if k == 0 else [normed_full]
        give, rest = hidden(direct, gathered[k][0], gathered[k][1], w_gate, w_up, nz, late)
        pair = (rest + swap(give).astype(f32)).astype(bf16)
        grad_normed = pair[0].astype(f32)
        for s in range(1, nz):
            grad_normed = grad_normed + z_step(pair[s], s).astype(f32)
        scaled.append(grad_normed * norm_gain[None, :])

    normed_full = normed_full.reshape(nz, 2, CHUNKS, sub, feat).transpose(2, 0, 1, 3, 4)
    normed_full = normed_full.reshape(total, feat)
    grad_gate = over_tokens(
        normed_full, jnp.concatenate([g[0] for g in gathered], axis=0)
    ).astype(bf16)
    grad_up = over_tokens(normed_full, jnp.concatenate([g[1] for g in gathered], axis=0)).astype(bf16)

    scaled = jnp.concatenate(scaled, axis=0)
    inner = row_total(jnp.sum(scaled * xs, axis=1)) / D
    branch = recip[:, None] * (scaled - xs * (recip * recip * inner)[:, None])
    grad_in = (grad_out.astype(f32) + branch).astype(bf16)
    return (grad_in, grad_gate, grad_up, grad_down)


def solution(mesh):
    return jax.shard_map(
        per_device,
        mesh=mesh,
        in_specs=(
            P("col", "row"),
            P("col", "row"),
            P("row", "col"),
            P("row", "col"),
            P("row", "col"),
            P("row"),
            P("row"),
            P("row", "col"),
            P("row", "col"),
            P("col", "row"),
        ),
        out_specs=(P("col", "row"), P("row", "col"), P("row", "col"), P("col", "row")),
        check_vma=False,
    )
```

time: 535 us -> 302 us (0.56); the launches traced: 527 us -> 300 us
  waiting for transfers between devices: 314 us -> 99.7 us
  Pallas kernels: 0 us -> 59.8 us
  starting transfers between devices: 7.49 us -> 63.4 us
  matrix products: 77.3 us -> 32.4 us
  other arithmetic: 51.4 us -> 8.11 us
  blocking collectives: 36.4 us -> 0 us
  between operations: 14.7 us -> 1.17 us
  local copies, waits for them, and re-layouts: 24.9 us -> 35.9 us
    reduce_scatter x2 -> x0, waiting for transfers between devices: 156 us -> none  [the longest x1 89.1 us: per_device(): lax.psum_scatter(over_width(gpre_full, w_gate) + over_width(upre_full, w_...]
    all_gather x5 -> x0, waiting for transfers between devices: 137 us -> none  [the longest x1 51.5 us: per_device(): lax.all_gather(grad_out, 'col', axis=0, tiled=True)]
    ppermute x0 -> x44, waiting for transfers between devices: none -> 99.7 us  [the longest x12 48.4 us: z_step(): return lax.ppermute(a, 'col', [(i, i ^ 2 * s) for i in range(n_col)])]
    ppermute x0 -> x44, starting transfers between devices: none -> 63.4 us  [the longest x24 30.5 us: row_step(): return lax.ppermute(a, 'row', [(i, i ^ j) for i in range(n_row)])]
    pallas_call x0 -> x11, Pallas kernels: none -> 59.8 us  [the longest x2 24.6 us: hidden(): pl.pallas_call(functools.partial(hidden_kernel, n), out_shape=(jax.ShapeD...]
    dot_general x3 -> x0, matrix products: 41.2 us -> none  [over_width(): lax.dot_general(left, right, (((1,), (1,)), ((), ())), preferred_element_...]
    unnamed x1 -> x0, other arithmetic: 38.5 us -> none
    all_to_all x1 -> x0, blocking collectives: 26.4 us -> none  [per_device(): lax.all_to_all(xs.reshape(n_row, per_dev, feat_loc), 'row', split_axis=0,...]
  transfers between devices with their start and end apart: 9 -> 44, of which waited for: 6 -> 12; matrix products, arithmetic and copies ran while one was open for 18% -> 21% of each run, Pallas kernels for 0% -> 20%
where the time goes in v1:
time: 302 us; the launch traced here: 300 us
  waiting for transfers between devices  99.7 us (33%)
  starting transfers between devices  63.4 us (21%)
  Pallas kernels  59.8 us (20%)
  local copies, waits for them, and re-layouts  35.9 us (12%)
  matrix products  32.4 us (11%)
  other arithmetic  8.11 us (3%)
    ppermute x12, waiting for transfers between devices, z_step(): return lax.ppermute(a, 'col', [(i, i ^ 2 * s) for i in range(n_col)])  48.4 us
    ppermute x24, waiting for transfers between devices, row_step(): return lax.ppermute(a, 'row', [(i, i ^ j) for i in range(n_row)])  41.1 us
    dot_general x3, matrix products, over_tokens(): lax.dot_general(left, right, (((0,), (0,)), ((), ())), preferred_element_...  32.4 us
    ppermute x24, starting transfers between devices, row_step(): return lax.ppermute(a, 'row', [(i, i ^ j) for i in range(n_row)])  30.5 us
    ppermute x12, starting transfers between devices, z_step(): return lax.ppermute(a, 'col', [(i, i ^ 2 * s) for i in range(n_col)])  26.2 us
    pallas_call x2, Pallas kernels, hidden(): pl.pallas_call(functools.partial(hidden_kernel, n), out_shape=(jax.ShapeD...  24.6 us
    unnamed x83, local copies, waits for them, and re-layouts  21.3 us
    pallas_call x2, Pallas kernels, back(): pl.pallas_call(functools.partial(back_kernel, n), out_shape=(jax.ShapeDty...  15.2 us
  transfers between devices with their start and end apart: 44, of which 12 were waited for; matrix products, arithmetic and copies ran while one was open for 21% of the time, Pallas kernels for 20%

profile of v1, /device:TPU:0, one launch (start us, length us, event | category | flops | bytes accessed | tf_op | source)
XLA Modules:
  0.0 300.5 jit_solution(3284596502488243452)
XLA Ops:
  2.7 4.0 %collective-permute-start.2 = (f32[144]{0:T(256)S(1)}, f32[144]{0:T(256)S(1)}, u32[]{:S(2)}, u32[]{:S(2)}) collective-permute-start(f32[144]{0:T(256)S(1)} %pad_maximum_fusion.5), channel_id=1, source_target_pairs={{0,24},{8,16},{16,8},{24,0},{1,25},{9,17},{17,9},{25,1},{2,26},{10... | collective-permute-start | bytes 1736 | tf_op jit(solution)/shard_map/ppermute | solution.py:277
  8.3 2.0 collective-permute-start.3
  10.4 2.6 collective-permute-start.4
  15.6 5.7 %shard_map.132 = bf16[2,128,1792]{2,1,0:T(8,128)(2,1)} custom-call(bf16[2,2,64,1792]{3,2,1,0:T(8,128)(2,1)} %bitcast.134, bf16[2,2,64,1792]{3,2,1,0:T(8,128)(2,1)} %bitcast.137, s32[2,2,64,1792]{3,2,1,0:T(8,128)} %bitcast.131, f32[2,2,64,1]{3,2,1,0:T(8,128)} %reshape.51.refs_7_.weight_ref), custom_call_target="tpu_custom_call" | custom-call | flops 4587520 | bytes 4587520 | tf_op jit(solution)/shard_map/pallas_call | solution.py:141
  26.3 5.5 %collective-permute-done.4.refs_2_ = bf16[64,2048]{1,0:T(8,128)(2,1)S(1)} collective-permute-done((bf16[64,2048]{1,0:T(8,128)(2,1)S(1)}, bf16[64,2048]{1,0:T(8,128)(2,1)S(1)}, u32[]{:S(2)}, u32[]{:S(2)}) %collective-permute-start.4) | collective-permute-done | bytes 262176 | tf_op jit(solution)/shard_map/ppermute | solution.py:271
  33.2 2.5 collective-permute-start.20
  42.0 23.5 %collective-permute-done.19.refs_2_ = bf16[64,2048]{1,0:T(8,128)(2,1)S(1)} collective-permute-done((bf16[64,2048]{1,0:T(8,128)(2,1)S(1)}, bf16[64,2048]{1,0:T(8,128)(2,1)S(1)}, u32[]{:S(2)}, u32[]{:S(2)}) %collective-permute-start.19) | collective-permute-done | bytes 262176 | tf_op jit(solution)/shard_map/ppermute | solution.py:271
  67.2 3.5 %collective-permute-start.23 = (bf16[128,2048]{1,0:T(8,128)(2,1)S(1)}, bf16[128,2048]{1,0:T(8,128)(2,1)S(1)}, u32[]{:S(2)}, u32[]{:S(2)}) collective-permute-start(bf16[128,2048]{1,0:T(8,128)(2,1)S(1)} %collective-permute-done.22.refs_10_.refs_1_), channel_id=1, source_target_pairs={{0,2},{1,3},{2,6},{3,7},{4,0},{5,1},{6,4},{7,5},{8,10},{9,11},{10,... | collective-permute-start | bytes 1572872 | tf_op jit(solution)/shard_map/ppermute | solution.py:274
  74.0 10.2 %collective-permute-done.23.refs_1_.refs_2_ = bf16[128,2048]{1,0:T(8,128)(2,1)S(1)} collective-permute-done((bf16[128,2048]{1,0:T(8,128)(2,1)S(1)}, bf16[128,2048]{1,0:T(8,128)(2,1)S(1)}, u32[]{:S(2)}, u32[]{:S(2)}) %collective-permute-start.23) | collective-permute-done | bytes 524320 | tf_op jit(solution)/shard_map/ppermute | solution.py:274
  84.9 7.2 %shard_map.130 = (bf16[4,2,64,2048]{3,2,1,0:T(8,128)(2,1)S(1)}, bf16[4,128,1792]{2,1,0:T(8,128)(2,1)S(1)}) custom-call(s32[5]{0:T(128)S(1)} %stack.39.where.where_ref, bf16[4,64,2048]{2,1,0:T(8,128)(2,1)S(1)} %shard_map.129.mine, bf16[4,64,2048]{2,1,0:T(8,128)(2,1)S(1)} %collective-permute-done.6.other, bf16[1792,2048]{1,0:T(8,128)(2,1)} %w_ref.3), custom_call_target="tpu_custom_call" | custom-call | flops 3758096384 | bytes 13369344 | tf_op jit(solution)/shard_map/pallas_call | solution.py:100
  96.2 8.1 %shard_map.134 = (bf16[4,2,64,2048]{3,2,1,0:T(8,128)(2,1)}, bf16[4,128,1792]{2,1,0:T(8,128)(2,1)S(1)}) custom-call(s32[5]{0:T(128)S(1)} %stack.39.where.where_ref, bf16[4,64,2048]{2,1,0:T(8,128)(2,1)S(1)} %shard_map.133.mine, bf16[4,64,2048]{2,1,0:T(8,128)(2,1)S(1)} %collective-permute-done.21.other, bf16[1792,2048]{1,0:T(8,128)(2,1)} %w_ref.3, ...), custom_call_target="tpu_custom_call" | custom-call | flops 3758096384 | bytes 13369344 | tf_op jit(solution)/shard_map/pallas_call | solution.py:100
  111.4 11.9 %convolution_convert_fusion.2.refs_0_ = bf16[1792,2048]{1,0:T(8,128)(2,1)} fusion(bf16[1024,1792]{1,0:T(8,128)(2,1)} %constant_dynamic-update-slice_fusion, bf16[512,2048]{1,0:T(8,128)(2,1)S(1)} %bitcast.142, bf16[512,2048]{1,0:T(8,128)(2,1)S(1)} %bitcast.130), kind=kOutput, calls=%fused_computation.2 | convolution fusion | flops 7528251392 | bytes 15204352 | tf_op jit(solution)/shard_map/dot_general | solution.py:22
  125.6 5.8 %shard_map.131 = bf16[2,128,1792]{2,1,0:T(8,128)(2,1)} custom-call(bf16[4,128,1792]{2,1,0:T(8,128)(2,1)} %copy-done.2, bf16[128,1792]{1,0:T(8,128)(2,1)} %collective-permute-done.7.refs_1_, bf16[128,1792]{1,0:T(8,128)(2,1)} %collective-permute-done.8.refs_2_, bf16[128,1792]{1,0:T(8,128)(2,1)} %collective-permute-done.9.refs_3_, ...), custom_call_target="tpu_custom_call" | custom-call | flops 4587520 | bytes 4587520 | tf_op jit(solution)/shard_map/pallas_call | solution.py:180
  132.9 2.2 slice_bitcast_fusion.14
  136.6 10.2 %collective-permute-done.30.refs_2_ = bf16[128,1792]{1,0:T(8,128)(2,1)} collective-permute-done((bf16[128,1792]{1,0:T(8,128)(2,1)}, bf16[128,1792]{1,0:T(8,128)(2,1)}, u32[]{:S(2)}, u32[]{:S(2)}) %collective-permute-start.30) | collective-permute-done | bytes 458784 | tf_op jit(solution)/shard_map/ppermute | solution.py:277
  146.8 5.8 %shard_map.136 = bf16[2,128,1792]{2,1,0:T(8,128)(2,1)} custom-call(bf16[4,128,1792]{2,1,0:T(8,128)(2,1)} %copy-done.1, bf16[128,1792]{1,0:T(8,128)(2,1)} %collective-permute-done.29.refs_1_, bf16[128,1792]{1,0:T(8,128)(2,1)} %collective-permute-done.30.refs_2_, bf16[128,1792]{1,0:T(8,128)(2,1)} %collective-permute-done.31.refs_3_, ...), custom_call_target="tpu_custom_call" | custom-call | flops 4587520 | bytes 4587520 | tf_op jit(solution)/shard_map/pallas_call | solution.py:180
  160.3 6.2 %collective-permute-done.11 = bf16[2,128,1792]{2,1,0:T(8,128)(2,1)} collective-permute-done((bf16[2,128,1792]{2,1,0:T(8,128)(2,1)}, bf16[2,128,1792]{2,1,0:T(8,128)(2,1)}, u32[]{:S(2)}, u32[]{:S(2)}) %collective-permute-start.11) | collective-permute-done | bytes 917536 | tf_op jit(solution)/shard_map/ppermute | solution.py:277
  168.4 8.7 %collective-permute-done.32 = bf16[2,128,1792]{2,1,0:T(8,128)(2,1)S(1)} collective-permute-done((bf16[2,128,1792]{2,1,0:T(8,128)(2,1)}, bf16[2,128,1792]{2,1,0:T(8,128)(2,1)S(1)}, u32[]{:S(2)}, u32[]{:S(2)}) %collective-permute-start.32) | collective-permute-done | bytes 917536 | tf_op jit(solution)/shard_map/ppermute | solution.py:277
  178.7 7.3 %collective-permute-done.33 = bf16[2,128,1792]{2,1,0:T(8,128)(2,1)S(1)} collective-permute-done((bf16[2,128,1792]{2,1,0:T(8,128)(2,1)}, bf16[2,128,1792]{2,1,0:T(8,128)(2,1)S(1)}, u32[]{:S(2)}, u32[]{:S(2)}) %collective-permute-start.33) | collective-permute-done | bytes 917536 | tf_op jit(solution)/shard_map/ppermute | solution.py:277
  189.3 6.6 %collective-permute-done.12 = bf16[128,1792]{1,0:T(8,128)(2,1)S(1)} collective-permute-done((bf16[128,1792]{1,0:T(8,128)(2,1)S(1)}, bf16[128,1792]{1,0:T(8,128)(2,1)S(1)}, u32[]{:S(2)}, u32[]{:S(2)}) %collective-permute-start.12) | collective-permute-done | bytes 458784 | tf_op jit(solution)/shard_map/ppermute | solution.py:277
  197.1 12.3 %shard_map.135 = (bf16[4,64,2048]{2,1,0:T(8,128)(2,1)S(1)}, f32[4,64,2048]{2,1,0:T(8,128)}) custom-call(s32[5]{0:T(128)S(1)} %stack.39.where.where_ref, bf16[512,1792]{1,0:T(8,128)(2,1)S(1)} %pad_maximum_fusion.gpre_ref, bf16[512,1792]{1,0:T(8,128)(2,1)S(1)} %pad_maximum_fusion.1.upre_ref, bf16[2048,1792]{1,0:T(8,128)(2,1)} %wg_ref.3, ...), custom_call_target="tpu_custom_call" | custom-call | flops 7516192768 | bytes 21495808 | tf_op jit(solution)/shard_map/pallas_call | solution.py:215
  215.1 2.2 shard_map.138.refs_0_
  219.3 12.3 %shard_map.139 = (bf16[4,64,2048]{2,1,0:T(8,128)(2,1)S(1)}, f32[4,64,2048]{2,1,0:T(8,128)}) custom-call(s32[5]{0:T(128)S(1)} %stack.39.where.where_ref, bf16[512,1792]{1,0:T(8,128)(2,1)S(1)} %pad_maximum_fusion.2.gpre_ref, bf16[512,1792]{1,0:T(8,128)(2,1)S(1)} %pad_maximum_fusion.3.upre_ref, bf16[2048,1792]{1,0:T(8,128)(2,1)} %wg_ref.3, ...), custom_call_target="tpu_custom_call" | custom-call | flops 7516192768 | bytes 21495808 | tf_op jit(solution)/shard_map/pallas_call | solution.py:215
  232.2 2.6 copy.21
  236.8 2.5 collective-permute-start.28
  241.6 2.5 collective-permute-start.40
  244.1 3.8 %collective-permute-done.28 = bf16[64,2048]{1,0:T(8,128)(2,1)S(1)} collective-permute-done((bf16[64,2048]{1,0:T(8,128)(2,1)S(1)}, bf16[64,2048]{1,0:T(8,128)(2,1)S(1)}, u32[]{:S(2)}, u32[]{:S(2)}) %collective-permute-start.28) | collective-permute-done | bytes 262176 | tf_op jit(solution)/shard_map/ppermute | solution.py:271
  248.0 11.3 %collective-permute-start.38 = (bf16[64,2048]{1,0:T(8,128)(2,1)S(1)}, bf16[64,2048]{1,0:T(8,128)(2,1)S(1)}, u32[]{:S(2)}, u32[]{:S(2)}) collective-permute-start(bf16[64,2048]{1,0:T(8,128)(2,1)S(1)} %get-tuple-element.29), channel_id=1, source_target_pairs={{0,2},{1,3},{2,0},{3,1},{4,6},{5,7},{6,4},{7,5},{8,10},{9,11},{10,... | collective-permute-start | bytes 786440 | tf_op jit(solution)/shard_map/ppermute | solution.py:271
  259.2 10.3 %convolution_convert_fusion.1 = bf16[2048,1792]{1,0:T(8,128)(2,1)} fusion(bf16[1024,2048]{1,0:T(8,128)(2,1)S(1)} %bitcast.140, bf16[1024,1792]{1,0:T(8,128)(2,1)S(1)} %copy-done.30), kind=kOutput, calls=%fused_computation.1 | convolution fusion | flops 7519862784 | bytes 15204352 | tf_op jit(solution)/shard_map/dot_general | solution.py:22
  269.5 5.3 %collective-permute-done.27 = bf16[64,2048]{1,0:T(8,128)(2,1)S(1)} collective-permute-done((bf16[64,2048]{1,0:T(8,128)(2,1)S(1)}, bf16[64,2048]{1,0:T(8,128)(2,1)S(1)}, u32[]{:S(2)}, u32[]{:S(2)}) %collective-permute-start.27) | collective-permute-done | bytes 262176 | tf_op jit(solution)/shard_map/ppermute | solution.py:271
  274.8 10.3 %collective-permute-done.39 = bf16[64,2048]{1,0:T(8,128)(2,1)S(1)} collective-permute-done((bf16[64,2048]{1,0:T(8,128)(2,1)S(1)}, bf16[64,2048]{1,0:T(8,128)(2,1)S(1)}, u32[]{:S(2)}, u32[]{:S(2)}) %collective-permute-start.39) | collective-permute-done | bytes 262176 | tf_op jit(solution)/shard_map/ppermute | solution.py:271
  289.2 10.1 %convolution_convert_fusion = bf16[2048,1792]{1,0:T(8,128)(2,1)} fusion(bf16[1024,2048]{1,0:T(8,128)(2,1)S(1)} %bitcast.141, bf16[1024,1792]{1,0:T(8,128)(2,1)S(1)} %constant_dynamic-update-slice_fusion.12), kind=kOutput, calls=%fused_computation | convolution fusion | flops 7519862784 | bytes 15204352 | tf_op jit(solution)/shard_map/dot_general | solution.py:22
  (191 shorter events, 74.2 us)
Async XLA Ops:
  10.4 21.4 %collective-permute-start.4 = (bf16[64,2048]{1,0:T(8,128)(2,1)S(1)}, bf16[64,2048]{1,0:T(8,128)(2,1)S(1)}, u32[]{:S(2)}, u32[]{:S(2)}) collective-permute-start(bf16[64,2048]{1,0:T(8,128)(2,1)S(1)} %get-tuple-element.56.refs_0_), channel_id=1, source_target_pairs={{0,4},{1,5},{2,6},{3,7},{4,0},{5,1},{6,2},{7,3},{8,12},{9,13},{10,... | collective-permute-start | bytes 786440 | tf_op jit(solution)/shard_map/ppermute | solution.py:271
  13.0 22.7 %collective-permute-start.18 = (bf16[64,2048]{1,0:T(8,128)(2,1)S(1)}, bf16[64,2048]{1,0:T(8,128)(2,1)S(1)}, u32[]{:S(2)}, u32[]{:S(2)}) collective-permute-start(bf16[64,2048]{1,0:T(8,128)(2,1)S(1)} %get-tuple-element.57.refs_0_), channel_id=1, source_target_pairs={{0,2},{1,3},{2,0},{3,1},{4,6},{5,7},{6,4},{7,5},{8,10},{9,11},{10,... | collective-permute-start | bytes 786440 | tf_op jit(solution)/shard_map/ppermute | solution.py:271
  21.3 49.3 %collective-permute-start.14 = (bf16[2,128,1792]{2,1,0:T(8,128)(2,1)}, bf16[2,128,1792]{2,1,0:T(8,128)(2,1)S(1)}, u32[]{:S(2)}, u32[]{:S(2)}) collective-permute-start(bf16[2,128,1792]{2,1,0:T(8,128)(2,1)} %shard_map.132), channel_id=1, source_target_pairs={{0,8},{8,0},{16,24},{24,16},{1,9},{9,1},{17,25},{25,17},{2,10},{10... | collective-permute-start | bytes 2752520 | tf_op jit(solution)/shard_map/ppermute | solution.py:277
  24.8 42.4 %collective-permute-start.22 = (bf16[128,2048]{1,0:T(8,128)(2,1)S(1)}, bf16[128,2048]{1,0:T(8,128)(2,1)S(1)}, u32[]{:S(2)}, u32[]{:S(2)}) collective-permute-start(bf16[128,2048]{1,0:T(8,128)(2,1)S(1)} %fusion.5.refs_0_), channel_id=1, source_target_pairs={{0,2},{1,3},{2,6},{3,7},{4,0},{5,1},{6,4},{7,5},{8,10},{9,11},{10,... | collective-permute-start | bytes 1572872 | tf_op jit(solution)/shard_map/ppermute | solution.py:274
  32.5 33.0 %collective-permute-start.19 = (bf16[64,2048]{1,0:T(8,128)(2,1)S(1)}, bf16[64,2048]{1,0:T(8,128)(2,1)S(1)}, u32[]{:S(2)}, u32[]{:S(2)}) collective-permute-start(bf16[64,2048]{1,0:T(8,128)(2,1)S(1)} %get-tuple-element.57.refs_0_), channel_id=1, source_target_pairs={{0,4},{1,5},{2,6},{3,7},{4,0},{5,1},{6,2},{7,3},{8,12},{9,13},{10,... | collective-permute-start | bytes 786440 | tf_op jit(solution)/shard_map/ppermute | solution.py:271
  33.2 32.3 %collective-permute-start.20 = (bf16[64,2048]{1,0:T(8,128)(2,1)S(1)}, bf16[64,2048]{1,0:T(8,128)(2,1)S(1)}, u32[]{:S(2)}, u32[]{:S(2)}) collective-permute-start(bf16[64,2048]{1,0:T(8,128)(2,1)S(1)} %get-tuple-element.57.refs_0_), channel_id=1, source_target_pairs={{0,6},{1,7},{2,4},{3,5},{4,2},{5,3},{6,0},{7,1},{8,14},{9,15},{10,... | collective-permute-start | bytes 786440 | tf_op jit(solution)/shard_map/ppermute | solution.py:271
  36.4 35.9 %collective-permute-start.15 = (bf16[2,128,1792]{2,1,0:T(8,128)(2,1)}, bf16[2,128,1792]{2,1,0:T(8,128)(2,1)S(1)}, u32[]{:S(2)}, u32[]{:S(2)}) collective-permute-start(bf16[2,128,1792]{2,1,0:T(8,128)(2,1)} %shard_map.132), channel_id=1, source_target_pairs={{0,16},{8,24},{16,0},{24,8},{1,17},{9,25},{17,1},{25,9},{2,18},{10... | collective-permute-start | bytes 2752520 | tf_op jit(solution)/shard_map/ppermute | solution.py:277
  66.6 28.0 %collective-permute-start.21 = (bf16[4,64,2048]{2,1,0:T(8,128)(2,1)S(1)}, bf16[4,64,2048]{2,1,0:T(8,128)(2,1)S(1)}, u32[]{:S(2)}, u32[]{:S(2)}) collective-permute-start(bf16[4,64,2048]{2,1,0:T(8,128)(2,1)S(1)} %shard_map.133.mine), channel_id=1, source_target_pairs={{0,1},{1,0},{2,3},{3,2},{4,5},{5,4},{6,7},{7,6},{8,9},{9,8},{10,11... | collective-permute-start | bytes 3145736 | tf_op jit(solution)/shard_map/ppermute | solution.py:268
  70.7 34.7 %collective-permute-start.16 = (bf16[128,1792]{1,0:T(8,128)(2,1)S(1)}, bf16[128,1792]{1,0:T(8,128)(2,1)S(1)}, u32[]{:S(2)}, u32[]{:S(2)}) collective-permute-start(bf16[128,1792]{1,0:T(8,128)(2,1)S(1)} %slice_bitcast_fusion.10), channel_id=1, source_target_pairs={{0,16},{8,24},{16,0},{24,8},{1,17},{9,25},{17,1},{25,9},{2,18},{10... | collective-permute-start | bytes 1376264 | tf_op jit(solution)/shard_map/ppermute | solution.py:277
  72.3 36.7 %collective-permute-start.17 = (bf16[128,1792]{1,0:T(8,128)(2,1)S(1)}, bf16[128,1792]{1,0:T(8,128)(2,1)S(1)}, u32[]{:S(2)}, u32[]{:S(2)}) collective-permute-start(bf16[128,1792]{1,0:T(8,128)(2,1)S(1)} %slice_bitcast_fusion.6), channel_id=1, source_target_pairs={{0,8},{8,0},{16,24},{24,16},{1,9},{9,1},{17,25},{25,17},{2,10},{10... | collective-permute-start | bytes 1376264 | tf_op jit(solution)/shard_map/ppermute | solution.py:277
  84.2 39.1 %collective-permute-start.24 = (bf16[128,2048]{1,0:T(8,128)(2,1)S(1)}, bf16[128,2048]{1,0:T(8,128)(2,1)S(1)}, u32[]{:S(2)}, u32[]{:S(2)}) collective-permute-start(bf16[128,2048]{1,0:T(8,128)(2,1)S(1)} %collective-permute-done.23.refs_1_.refs_2_), channel_id=1, source_target_pairs={{0,2},{1,3},{2,6},{3,7},{4,0},{5,1},{6,4},{7,5},{8,10},{9,11},{10,... | collective-permute-start | bytes 1572872 | tf_op jit(solution)/shard_map/ppermute | solution.py:274
  93.1 31.9 %collective-permute-start.7 = (bf16[128,1792]{1,0:T(8,128)(2,1)}, bf16[128,1792]{1,0:T(8,128)(2,1)}, u32[]{:S(2)}, u32[]{:S(2)}) collective-permute-start(bf16[128,1792]{1,0:T(8,128)(2,1)} %get-tuple-element.22), channel_id=1, source_target_pairs={{0,8},{8,0},{16,24},{24,16},{1,9},{9,1},{17,25},{25,17},{2,10},{10... | collective-permute-start | bytes 1376264 | tf_op jit(solution)/shard_map/ppermute | solution.py:277
  94.6 31.0 %collective-permute-start.8 = (bf16[128,1792]{1,0:T(8,128)(2,1)S(1)}, bf16[128,1792]{1,0:T(8,128)(2,1)}, u32[]{:S(2)}, u32[]{:S(2)}) collective-permute-start(bf16[128,1792]{1,0:T(8,128)(2,1)S(1)} %get-tuple-element.21), channel_id=1, source_target_pairs={{0,16},{8,24},{16,0},{24,8},{1,17},{9,25},{17,1},{25,9},{2,18},{10... | collective-permute-start | bytes 1376264 | tf_op jit(solution)/shard_map/ppermute | solution.py:277
  105.4 20.2 %collective-permute-start.9 = (bf16[128,1792]{1,0:T(8,128)(2,1)S(1)}, bf16[128,1792]{1,0:T(8,128)(2,1)}, u32[]{:S(2)}, u32[]{:S(2)}) collective-permute-start(bf16[128,1792]{1,0:T(8,128)(2,1)S(1)} %get-tuple-element.20), channel_id=1, source_target_pairs={{0,24},{8,16},{16,8},{24,0},{1,25},{9,17},{17,9},{25,1},{2,26},{10... | collective-permute-start | bytes 1376264 | tf_op jit(solution)/shard_map/ppermute | solution.py:277
  109.1 26.0 %collective-permute-start.29 = (bf16[128,1792]{1,0:T(8,128)(2,1)}, bf16[128,1792]{1,0:T(8,128)(2,1)}, u32[]{:S(2)}, u32[]{:S(2)}) collective-permute-start(bf16[128,1792]{1,0:T(8,128)(2,1)} %get-tuple-element.25), channel_id=1, source_target_pairs={{0,8},{8,0},{16,24},{24,16},{1,9},{9,1},{17,25},{25,17},{2,10},{10... | collective-permute-start | bytes 1376264 | tf_op jit(solution)/shard_map/ppermute | solution.py:277
  123.3 23.6 %collective-permute-start.30 = (bf16[128,1792]{1,0:T(8,128)(2,1)}, bf16[128,1792]{1,0:T(8,128)(2,1)}, u32[]{:S(2)}, u32[]{:S(2)}) collective-permute-start(bf16[128,1792]{1,0:T(8,128)(2,1)} %get-tuple-element.24), channel_id=1, source_target_pairs={{0,16},{8,24},{16,0},{24,8},{1,17},{9,25},{17,1},{25,9},{2,18},{10... | collective-permute-start | bytes 1376264 | tf_op jit(solution)/shard_map/ppermute | solution.py:277
  125.1 21.8 %collective-permute-start.31 = (bf16[128,1792]{1,0:T(8,128)(2,1)}, bf16[128,1792]{1,0:T(8,128)(2,1)}, u32[]{:S(2)}, u32[]{:S(2)}) collective-permute-start(bf16[128,1792]{1,0:T(8,128)(2,1)} %get-tuple-element.23), channel_id=1, source_target_pairs={{0,24},{8,16},{16,8},{24,0},{1,25},{9,17},{17,9},{25,1},{2,26},{10... | collective-permute-start | bytes 1376264 | tf_op jit(solution)/shard_map/ppermute | solution.py:277
  125.6 89.5 %collective-permute-start.36 = (bf16[4,128,2048]{2,1,0:T(8,128)(2,1)S(1)}, bf16[4,128,2048]{2,1,0:T(8,128)(2,1)}, u32[]{:S(2)}, u32[]{:S(2)}) collective-permute-start(bf16[4,128,2048]{2,1,0:T(8,128)(2,1)S(1)} %shard_map.137.mine), channel_id=1, source_target_pairs={{0,1},{1,0},{2,3},{3,2},{4,5},{5,4},{6,7},{7,6},{8,9},{9,8},{10,11... | collective-permute-start | bytes 6291464 | tf_op jit(solution)/shard_map/ppermute | solution.py:268
  131.4 26.1 %collective-permute-start.10 = (bf16[2,128,1792]{2,1,0:T(8,128)(2,1)}, bf16[2,128,1792]{2,1,0:T(8,128)(2,1)}, u32[]{:S(2)}, u32[]{:S(2)}) collective-permute-start(bf16[2,128,1792]{2,1,0:T(8,128)(2,1)} %shard_map.131), channel_id=1, source_target_pairs={{0,8},{8,0},{16,24},{24,16},{1,9},{9,1},{17,25},{25,17},{2,10},{10... | collective-permute-start | bytes 2752520 | tf_op jit(solution)/shard_map/ppermute | solution.py:277
  135.1 31.4 %collective-permute-start.11 = (bf16[2,128,1792]{2,1,0:T(8,128)(2,1)}, bf16[2,128,1792]{2,1,0:T(8,128)(2,1)}, u32[]{:S(2)}, u32[]{:S(2)}) collective-permute-start(bf16[2,128,1792]{2,1,0:T(8,128)(2,1)} %shard_map.131), channel_id=1, source_target_pairs={{0,16},{8,24},{16,0},{24,8},{1,17},{9,25},{17,1},{25,9},{2,18},{10... | collective-permute-start | bytes 2752520 | tf_op jit(solution)/shard_map/ppermute | solution.py:277
  152.6 24.4 %collective-permute-start.32 = (bf16[2,128,1792]{2,1,0:T(8,128)(2,1)}, bf16[2,128,1792]{2,1,0:T(8,128)(2,1)S(1)}, u32[]{:S(2)}, u32[]{:S(2)}) collective-permute-start(bf16[2,128,1792]{2,1,0:T(8,128)(2,1)} %shard_map.136), channel_id=1, source_target_pairs={{0,8},{8,0},{16,24},{24,16},{1,9},{9,1},{17,25},{25,17},{2,10},{10... | collective-permute-start | bytes 2752520 | tf_op jit(solution)/shard_map/ppermute | solution.py:277
  153.2 32.8 %collective-permute-start.33 = (bf16[2,128,1792]{2,1,0:T(8,128)(2,1)}, bf16[2,128,1792]{2,1,0:T(8,128)(2,1)S(1)}, u32[]{:S(2)}, u32[]{:S(2)}) collective-permute-start(bf16[2,128,1792]{2,1,0:T(8,128)(2,1)} %shard_map.136), channel_id=1, source_target_pairs={{0,16},{8,24},{16,0},{24,8},{1,17},{9,25},{17,1},{25,9},{2,18},{10... | collective-permute-start | bytes 2752520 | tf_op jit(solution)/shard_map/ppermute | solution.py:277
  158.7 37.1 %collective-permute-start.12 = (bf16[128,1792]{1,0:T(8,128)(2,1)S(1)}, bf16[128,1792]{1,0:T(8,128)(2,1)S(1)}, u32[]{:S(2)}, u32[]{:S(2)}) collective-permute-start(bf16[128,1792]{1,0:T(8,128)(2,1)S(1)} %get-tuple-element.47), channel_id=1, source_target_pairs={{0,16},{8,24},{16,0},{24,8},{1,17},{9,25},{17,1},{25,9},{2,18},{10... | collective-permute-start | bytes 1376264 | tf_op jit(solution)/shard_map/ppermute | solution.py:277
  167.7 28.3 %collective-permute-start.13 = (bf16[128,1792]{1,0:T(8,128)(2,1)S(1)}, bf16[128,1792]{1,0:T(8,128)(2,1)S(1)}, u32[]{:S(2)}, u32[]{:S(2)}) collective-permute-start(bf16[128,1792]{1,0:T(8,128)(2,1)S(1)} %get-tuple-element.48), channel_id=1, source_target_pairs={{0,8},{8,0},{16,24},{24,16},{1,9},{9,1},{17,25},{25,17},{2,10},{10... | collective-permute-start | bytes 1376264 | tf_op jit(solution)/shard_map/ppermute | solution.py:277
  177.1 32.2 %collective-permute-start.34 = (bf16[128,1792]{1,0:T(8,128)(2,1)S(1)}, bf16[128,1792]{1,0:T(8,128)(2,1)S(1)}, u32[]{:S(2)}, u32[]{:S(2)}) collective-permute-start(bf16[128,1792]{1,0:T(8,128)(2,1)S(1)} %get-tuple-element.53), channel_id=1, source_target_pairs={{0,16},{8,24},{16,0},{24,8},{1,17},{9,25},{17,1},{25,9},{2,18},{10... | collective-permute-start | bytes 1376264 | tf_op jit(solution)/shard_map/ppermute | solution.py:277
  186.1 25.1 %collective-permute-start.35 = (bf16[128,1792]{1,0:T(8,128)(2,1)S(1)}, bf16[128,1792]{1,0:T(8,128)(2,1)S(1)}, u32[]{:S(2)}, u32[]{:S(2)}) collective-permute-start(bf16[128,1792]{1,0:T(8,128)(2,1)S(1)} %get-tuple-element.54), channel_id=1, source_target_pairs={{0,8},{8,0},{16,24},{24,16},{1,9},{9,1},{17,25},{25,17},{2,10},{10... | collective-permute-start | bytes 1376264 | tf_op jit(solution)/shard_map/ppermute | solution.py:277
  209.4 25.5 %collective-permute-start.25 = (bf16[4,64,2048]{2,1,0:T(8,128)(2,1)S(1)}, bf16[4,64,2048]{2,1,0:T(8,128)(2,1)}, u32[]{:S(2)}, u32[]{:S(2)}) collective-permute-start(bf16[4,64,2048]{2,1,0:T(8,128)(2,1)S(1)} %get-tuple-element.16), channel_id=1, source_target_pairs={{0,1},{1,0},{2,3},{3,2},{4,5},{5,4},{6,7},{7,6},{8,9},{9,8},{10,11... | collective-permute-start | bytes 3145736 | tf_op jit(solution)/shard_map/ppermute | solution.py:268
  239.3 35.5 %collective-permute-start.27 = (bf16[64,2048]{1,0:T(8,128)(2,1)S(1)}, bf16[64,2048]{1,0:T(8,128)(2,1)S(1)}, u32[]{:S(2)}, u32[]{:S(2)}) collective-permute-start(bf16[64,2048]{1,0:T(8,128)(2,1)S(1)} %get-tuple-element.28), channel_id=1, source_target_pairs={{0,4},{1,5},{2,6},{3,7},{4,0},{5,1},{6,2},{7,3},{8,12},{9,13},{10,... | collective-permute-start | bytes 786440 | tf_op jit(solution)/shard_map/ppermute | solution.py:271
  239.6 35.2 %collective-permute-start.26 = (bf16[64,2048]{1,0:T(8,128)(2,1)S(1)}, bf16[64,2048]{1,0:T(8,128)(2,1)S(1)}, u32[]{:S(2)}, u32[]{:S(2)}) collective-permute-start(bf16[64,2048]{1,0:T(8,128)(2,1)S(1)} %get-tuple-element.26), channel_id=1, source_target_pairs={{0,2},{1,3},{2,0},{3,1},{4,6},{5,7},{6,4},{7,5},{8,10},{9,11},{10,... | collective-permute-start | bytes 786440 | tf_op jit(solution)/shard_map/ppermute | solution.py:271
  241.6 33.2 %collective-permute-start.40 = (bf16[64,2048]{1,0:T(8,128)(2,1)S(1)}, bf16[64,2048]{1,0:T(8,128)(2,1)S(1)}, u32[]{:S(2)}, u32[]{:S(2)}) collective-permute-start(bf16[64,2048]{1,0:T(8,128)(2,1)S(1)} %get-tuple-element.30), channel_id=1, source_target_pairs={{0,6},{1,7},{2,4},{3,5},{4,2},{5,3},{6,0},{7,1},{8,14},{9,15},{10,... | collective-permute-start | bytes 786440 | tf_op jit(solution)/shard_map/ppermute | solution.py:271
  244.1 40.9 %collective-permute-start.39 = (bf16[64,2048]{1,0:T(8,128)(2,1)S(1)}, bf16[64,2048]{1,0:T(8,128)(2,1)S(1)}, u32[]{:S(2)}, u32[]{:S(2)}) collective-permute-start(bf16[64,2048]{1,0:T(8,128)(2,1)S(1)} %get-tuple-element.31), channel_id=1, source_target_pairs={{0,4},{1,5},{2,6},{3,7},{4,0},{5,1},{6,2},{7,3},{8,12},{9,13},{10,... | collective-permute-start | bytes 786440 | tf_op jit(solution)/shard_map/ppermute | solution.py:271
  248.0 37.1 %collective-permute-start.38 = (bf16[64,2048]{1,0:T(8,128)(2,1)S(1)}, bf16[64,2048]{1,0:T(8,128)(2,1)S(1)}, u32[]{:S(2)}, u32[]{:S(2)}) collective-permute-start(bf16[64,2048]{1,0:T(8,128)(2,1)S(1)} %get-tuple-element.29), channel_id=1, source_target_pairs={{0,2},{1,3},{2,0},{3,1},{4,6},{5,7},{6,4},{7,5},{8,10},{9,11},{10,... | collective-permute-start | bytes 786440 | tf_op jit(solution)/shard_map/ppermute | solution.py:271
  (46 other events, 507.1 us)

commit v2 on v1

v2 whole, which is shorter than its diff:
```python
import functools

import jax
import jax.numpy as jnp
from jax import lax
from jax.experimental import pallas as pl
from jax.experimental.pallas import tpu as pltpu
from jax.sharding import PartitionSpec as P

D = 8192
SEGS = 16
LANES = 128
VMEM = 60 * 1024 * 1024
CHUNKS = 2
SHARE = 8

eps = 1e-05
keep_scale = 1.0 / 0.9
bf16 = jnp.bfloat16
f32 = jnp.float32
ANY = pl.BlockSpec(memory_space=pl.ANY)


def cost(flops, bytes_accessed, transcendentals):
    return pl.CostEstimate(
        flops=flops // SHARE,
        bytes_accessed=bytes_accessed // SHARE,
        transcendentals=transcendentals // SHARE,
    )


def over_tokens(left, right):
    return lax.dot_general(left, right, (((0,), (0,)), ((), ())), preferred_element_type=f32)


def over_width(left, right):
    return lax.dot_general(left, right, (((1,), (1,)), ((), ())), preferred_element_type=f32)


def join_kernel(n, *refs):
    parts, out, sems = refs[:n], refs[-2], refs[-1]
    copies = [pltpu.make_async_copy(parts[s], out.at[s], sems.at[s]) for s in range(n)]
    for copy in copies:
        copy.start()
    for copy in copies:
        copy.wait()


def join(parts, after=()):
    n = len(parts)
    shape = (n,) + parts[0].shape
    return pl.pallas_call(
        functools.partial(join_kernel, n),
        out_shape=jax.ShapeDtypeStruct(shape, parts[0].dtype),
        in_specs=[ANY] * (n + len(after)),
        scratch_shapes=[pltpu.SemaphoreType.DMA((n,))],
        compiler_params=pltpu.CompilerParams(vmem_limit_bytes=VMEM),
        cost_estimate=cost(
            flops=0, bytes_accessed=4 * n * parts[0].size, transcendentals=0
        ),
    )(*parts, *after)


def fill(n, where, mine, other, out, sems):
    core = where[0]
    copies = []
    for s in range(n):
        copies.append(pltpu.make_async_copy(mine.at[s], out.at[where[1 + s], core], sems.at[s]))
        copies.append(
            pltpu.make_async_copy(other.at[s], out.at[where[1 + s], 1 - core], sems.at[n + s])
        )
    for copy in copies:
        copy.start()
    for copy in copies:
        copy.wait()


def gather_slots(plan, refs, out, sems, first):
    copies = []
    for at, (ref, half) in enumerate(plan):
        source = refs[ref] if half is None else refs[ref].at[half]
        copies.append(pltpu.make_async_copy(source, out.at[at], sems.at[first + at]))
    return copies


def take_kernel(n, a_ref, *refs):
    for s in range(n):
        refs[-1][s] = a_ref[...]


def take(a, k, sub, n, after=()):
    feat = a.shape[1]
    return pl.pallas_call(
        functools.partial(take_kernel, n),
        out_shape=jax.ShapeDtypeStruct((n, sub, feat), a.dtype),
        grid=(1,),
        in_specs=[pl.BlockSpec((sub, feat), lambda i: (k, 0))] + [ANY] * len(after),
        out_specs=pl.BlockSpec((n, sub, feat), lambda i: (0, 0, 0)),
        compiler_params=pltpu.CompilerParams(vmem_limit_bytes=VMEM),
        cost_estimate=cost(flops=0, bytes_accessed=2 * (n + 1) * sub * feat, transcendentals=0),
    )(a, *after)


def pick_kernel(a_ref, *refs):
    refs[-1][...] = a_ref[...]


def pick(a, h, after=()):
    shape = a.shape[1:]
    return pl.pallas_call(
        pick_kernel,
        out_shape=jax.ShapeDtypeStruct(shape, a.dtype),
        grid=(1,),
        in_specs=[pl.BlockSpec((None,) + shape, lambda i: (h, 0, 0))] + [ANY] * len(after),
        out_specs=pl.BlockSpec(shape, lambda i: (0, 0)),
        compiler_params=pltpu.CompilerParams(vmem_limit_bytes=VMEM),
        cost_estimate=cost(flops=0, bytes_accessed=2 * a.size, transcendentals=0),
    )(a, *after)


def hold_kernel(a_ref, *refs):
    refs[-1][...] = a_ref[...]


def hold(a, after):
    whole = pl.BlockSpec(a.shape, lambda i: (0, 0, 0))
    return pl.pallas_call(
        hold_kernel,
        out_shape=jax.ShapeDtypeStruct(a.shape, a.dtype),
        grid=(1,),
        in_specs=[whole] + [ANY] * len(after),
        out_specs=whole,
        compiler_params=pltpu.CompilerParams(vmem_limit_bytes=VMEM),
        cost_estimate=cost(flops=0, bytes_accessed=4 * a.size, transcendentals=0),
    )(a, *after)


def normed_kernel(n, x_ref, recip_ref, gain_ref, *refs):
    normed = (x_ref[...].astype(f32) * recip_ref[...] * gain_ref[...]).astype(bf16)
    for s in range(n):
        refs[-1][s] = normed


def normalize(x, recip, gain, n, after=()):
    return pl.pallas_call(
        functools.partial(normed_kernel, n),
        out_shape=jax.ShapeDtypeStruct((n,) + x.shape, bf16),
        grid=(1,),
        in_specs=[pl.BlockSpec(a.shape, lambda i: (0, 0)) for a in (x, recip, gain)]
        + [ANY] * len(after),
        out_specs=pl.BlockSpec((n,) + x.shape, lambda i: (0, 0, 0)),
        compiler_params=pltpu.CompilerParams(vmem_limit_bytes=VMEM),
        cost_estimate=cost(
            flops=2 * x.size, bytes_accessed=2 * (n + 1) * x.size, transcendentals=0
        ),
    )(x, recip, gain, *after)


def pair_kernel(rest_ref, got_ref, *refs):
    refs[-1][...] = (rest_ref[...] + got_ref[...].astype(f32)).astype(bf16)


def add_pair(rest, got, after=()):
    whole = pl.BlockSpec(rest.shape, lambda i: (0, 0, 0))
    return pl.pallas_call(
        pair_kernel,
        out_shape=jax.ShapeDtypeStruct(rest.shape, bf16),
        grid=(1,),
        in_specs=[whole, whole] + [ANY] * len(after),
        out_specs=whole,
        compiler_params=pltpu.CompilerParams(vmem_limit_bytes=VMEM),
        cost_estimate=cost(flops=rest.size, bytes_accessed=8 * rest.size, transcendentals=0),
    )(rest, got, *after)


def settle_kernel(parts, gain, x, *refs):
    scaled_ref, inner_ref = refs[-2:]
    total = jnp.sum(parts[...].astype(f32), axis=0)
    scaled = total * gain[...]
    scaled_ref[...] = scaled
    inner = jnp.sum(scaled * x[...].astype(f32), axis=1, keepdims=True)
    inner_ref[...] = jnp.broadcast_to(inner, inner_ref.shape)


def settle(k, parts, gain, x, after=()):
    n, sub, feat = parts.shape
    block = pl.BlockSpec((sub, feat), lambda i: (0, 0))
    return pl.pallas_call(
        settle_kernel,
        out_shape=(
            jax.ShapeDtypeStruct((sub, feat), f32),
            jax.ShapeDtypeStruct((sub, LANES), f32),
        ),
        grid=(1,),
        in_specs=[
            pl.BlockSpec((n, sub, feat), lambda i: (0, 0, 0)),
            pl.BlockSpec((1, feat), lambda i: (0, 0)),
            pl.BlockSpec((sub, feat), lambda i: (k, 0)),
        ]
        + [ANY] * len(after),
        out_specs=(block, pl.BlockSpec((sub, LANES), lambda i: (0, 0))),
        compiler_params=pltpu.CompilerParams(vmem_limit_bytes=VMEM),
        cost_estimate=cost(
            flops=6 * sub * feat, bytes_accessed=14 * sub * feat, transcendentals=0
        ),
    )(parts, gain, x, *after)


def weight_grads_kernel(n, plan, count, where, mine, other, *refs):
    rights = refs[:count]
    left, right, sems = refs[-3:]
    gate_ref, up_ref = refs[-5:-3]
    sub = left.shape[3]
    step, tile = pl.program_id(0), gate_ref.shape[0]

    @pl.when(step == 0)
    def _():
        core = where[0]
        copies = []
        for s in range(n):
            for k in range(CHUNKS):
                rows = pl.ds(k * sub, sub)
                at = where[1 + s]
                copies.append((mine.at[s, rows], left.at[k, at, core]))
                copies.append((other.at[s, rows], left.at[k, at, 1 - core]))
        copies = [pltpu.make_async_copy(a, b, sems.at[i]) for i, (a, b) in enumerate(copies)]
        copies += gather_slots(plan, rights, right, sems, len(copies))
        for copy in copies:
            copy.start()
        for copy in copies:
            copy.wait()

    columns = pl.ds(pl.multiple_of(step * tile, tile), tile)
    a = left[:, :, :, :, columns].reshape(-1, tile)
    for q, out in enumerate((gate_ref, up_ref)):
        b = right[q * len(plan) // 2 : (q + 1) * len(plan) // 2].reshape(a.shape[0], -1)
        out[...] = over_tokens(a, b).astype(bf16)


def weight_grads(where, mine, other, slots, plan, after=()):
    n, tok, feat = mine.shape
    size, width = slots[0].shape[1:]
    tile = min(512, feat)
    tokens = 2 * n * tok
    return pl.pallas_call(
        functools.partial(weight_grads_kernel, n, plan, len(slots)),
        out_shape=(jax.ShapeDtypeStruct((feat, width), bf16),) * 2,
        grid=(feat // tile,),
        in_specs=[pl.BlockSpec(memory_space=pltpu.SMEM)] + [ANY] * (2 + len(slots) + len(after)),
        out_specs=(pl.BlockSpec((tile, width), lambda i: (i, 0)),) * 2,
        scratch_shapes=[
            pltpu.VMEM((CHUNKS, n, 2, tok // CHUNKS, feat), bf16),
            pltpu.VMEM((len(plan), size, width), bf16),
            pltpu.SemaphoreType.DMA((2 * n * CHUNKS + len(plan),)),
        ],
        compiler_params=pltpu.CompilerParams(vmem_limit_bytes=VMEM),
        cost_estimate=cost(
            flops=4 * tokens * width * feat,
            bytes_accessed=2 * (tokens * feat + 2 * tokens * width + 2 * width * feat),
            transcendentals=0,
        ),
    )(where, mine, other, *slots, *after)


def back_kernel(n, where, mine, other, w_ref, *refs):
    cot, parts, sems = refs[-n - 2], refs[-n - 1 : -1], refs[-1]
    size = 2 * cot.shape[2]

    @pl.when(pl.program_id(0) == 0)
    def _():
        fill(n, where, mine, other, cot, sems)

    left = cot[...].reshape(-1, cot.shape[-1])
    out = over_width(left, w_ref[...]).astype(bf16)
    for j in range(n):
        parts[j][:size] = out[j * size : (j + 1) * size]
        if parts[j].shape[0] > size:
            parts[j][size:] = refs[0][...]


def back(where, mine, other, w_down, more, after=()):
    n, sub, feat = mine.shape
    size = 2 * sub + sum(a.shape[0] for a in more)
    width = w_down.shape[0]
    tile = width // 2 if width // 2 % 128 == 0 else width
    tokens = 2 * n * sub
    return pl.pallas_call(
        functools.partial(back_kernel, n),
        out_shape=(
            jax.ShapeDtypeStruct((n, 2, sub, feat), bf16),
        )
        + (jax.ShapeDtypeStruct((size, width), bf16),) * n,
        grid=(width // tile,),
        in_specs=[
            pl.BlockSpec(memory_space=pltpu.SMEM),
            ANY,
            ANY,
            pl.BlockSpec((tile, feat), lambda i: (i, 0)),
        ]
        + [pl.BlockSpec((a.shape[0], tile), lambda i: (0, i)) for a in more]
        + [ANY] * len(after),
        out_specs=(
            pl.BlockSpec((n, 2, sub, feat), lambda i: (0, 0, 0, 0)),
        )
        + (pl.BlockSpec((size, tile), lambda i: (0, i)),) * n,
        scratch_shapes=[pltpu.SemaphoreType.DMA((2 * n,))],
        compiler_params=pltpu.CompilerParams(vmem_limit_bytes=VMEM),
        cost_estimate=cost(
            flops=2 * tokens * width * feat,
            bytes_accessed=2 * (2 * tokens * feat + width * feat + tokens * width),
            transcendentals=0,
        ),
    )(where, mine, other, w_down, *more, *after)


def masked_kernel(gate_ref, up_ref, keep_ref, *outs):
    for k in range(CHUNKS):
        gate = gate_ref[:, k].astype(f32)
        scale = keep_ref[:, k].astype(f32) * keep_scale
        value = gate * jax.nn.sigmoid(gate) * up_ref[:, k].astype(f32) * scale
        outs[k][...] = value.astype(bf16).reshape(outs[k].shape)


def masked(gate, up, keep):
    two, chunks, sub, width = gate.shape
    tile = width // 2 if width // 2 % 128 == 0 else width
    return pl.pallas_call(
        masked_kernel,
        out_shape=(jax.ShapeDtypeStruct((two * sub, width), bf16),) * chunks,
        grid=(width // tile,),
        in_specs=[pl.BlockSpec((two, chunks, sub, tile), lambda i: (0, 0, 0, i))] * 3,
        out_specs=(pl.BlockSpec((two * sub, tile), lambda i: (0, i)),) * chunks,
        compiler_params=pltpu.CompilerParams(vmem_limit_bytes=VMEM),
        cost_estimate=cost(
            flops=10 * gate.size, bytes_accessed=10 * gate.size, transcendentals=gate.size
        ),
    )(gate, up, keep)


def grads_kernel(n, *refs):
    parts = refs[:n]
    gate_ref, up_ref, keep_ref, weight_ref = refs[n : n + 4]
    out = refs[-1]
    total = parts[0][...].astype(f32)
    for part in parts[1:]:
        total = total + part[...].astype(f32)
    two, sub, tile = gate_ref.shape
    total = total.reshape(two, sub, tile)
    gate, up = gate_ref[...].astype(f32), up_ref[...].astype(f32)
    act = total * (keep_ref[...].astype(f32) * keep_scale * weight_ref[...])
    sig = jax.nn.sigmoid(gate)
    gpre = act * up * sig * (1.0 + gate * (1.0 - sig))
    out[0] = gpre.astype(bf16).reshape(out.shape[1:])
    out[1] = (act * gate * sig).astype(bf16).reshape(out.shape[1:])


def hidden_grads(k, parts, gate, up, keep, weights, after=()):
    n = len(parts)
    two, chunks, sub, width = gate.shape
    tile = width // 2 if width // 2 % 128 == 0 else width
    block = pl.BlockSpec((two, None, sub, tile), lambda i: (0, k, 0, i))
    size = two * sub * width
    return pl.pallas_call(
        functools.partial(grads_kernel, n),
        out_shape=jax.ShapeDtypeStruct((2, two * sub, width), bf16),
        grid=(width // tile,),
        in_specs=[pl.BlockSpec((two * sub, tile), lambda i: (0, i))] * n
        + [block] * 3
        + [pl.BlockSpec((two, None, sub, 1), lambda i: (0, k, 0, 0))]
        + [ANY] * len(after),
        out_specs=pl.BlockSpec((2, two * sub, tile), lambda i: (0, 0, i)),
        compiler_params=pltpu.CompilerParams(vmem_limit_bytes=VMEM),
        cost_estimate=cost(
            flops=20 * size, bytes_accessed=(12 + 2 * n) * size, transcendentals=size
        ),
    )(*parts, gate, up, keep, weights, *after)


def hidden_kernel(n, plan, count, where, *refs):
    slots, (wg_ref, wu_ref) = refs[:count], refs[count : count + 2]
    give_ref, keep_ref, left, sems = refs[-4:]

    @pl.when(pl.program_id(0) == 0)
    def _():
        copies = gather_slots(plan, slots, left, sems, 0)
        for copy in copies:
            copy.start()
        for copy in copies:
            copy.wait()

    half = len(plan) // 2
    width = left.shape[2]
    gpre = left[:half].reshape(-1, width)
    upre = left[half:].reshape(-1, width)
    part = over_width(gpre, wg_ref[...]) + over_width(upre, wu_ref[...])
    sub = give_ref.shape[1]
    part = part.reshape(n, 2, sub, part.shape[1])
    low = where[0] == 0
    for j in range(n):
        at = where[1 + j]
        keep_ref[at] = jnp.where(low, part[j, 0], part[j, 1])
        give_ref[at] = jnp.where(low, part[j, 1], part[j, 0]).astype(bf16)


def hidden(where, slots, plan, w_gate, w_up, n, after=()):
    size, width = slots[0].shape[1:]
    feat = w_gate.shape[0]
    tile = min(512, feat)
    tokens = len(plan) // 2 * size
    sub = tokens // (2 * n)
    return pl.pallas_call(
        functools.partial(hidden_kernel, n, plan, len(slots)),
        out_shape=(
            jax.ShapeDtypeStruct((n, sub, feat), bf16),
            jax.ShapeDtypeStruct((n, sub, feat), f32),
        ),
        grid=(feat // tile,),
        in_specs=[pl.BlockSpec(memory_space=pltpu.SMEM)]
        + [ANY] * len(slots)
        + [pl.BlockSpec((tile, width), lambda i: (i, 0))] * 2
        + [ANY] * len(after),
        out_specs=(pl.BlockSpec((n, sub, tile), lambda i: (0, 0, i)),) * 2,
        scratch_shapes=[
            pltpu.VMEM((len(plan), size, width), bf16),
            pltpu.SemaphoreType.DMA((len(plan),)),
        ],
        compiler_params=pltpu.CompilerParams(vmem_limit_bytes=VMEM),
        cost_estimate=cost(
            flops=4 * tokens * width * feat,
            bytes_accessed=4 * width * (tokens + feat) + 6 * n * sub * feat,
            transcendentals=0,
        ),
    )(where, *slots, w_gate, w_up, *after)


def down_grad_kernel(plan, count, weight_ref, *refs):
    drops, cots = refs[:count], refs[count : count + CHUNKS]
    out, left, right, sems = refs[-4:]
    step, tile = pl.program_id(0), out.shape[0]

    @pl.when(step == 0)
    def _():
        copies = gather_slots(plan, drops, left, sems, 0)
        for k in range(CHUNKS):
            copies.append(pltpu.make_async_copy(cots[k], right.at[k], sems.at[len(plan) + k]))
        for copy in copies:
            copy.start()
        for copy in copies:
            copy.wait()

    columns = pl.ds(pl.multiple_of(step * tile, tile), tile)
    a = left[:, :, columns].astype(f32) * weight_ref[...]
    a = a.astype(bf16).reshape(-1, tile)
    out[...] = over_tokens(a, right[...].reshape(a.shape[0], -1)).astype(bf16)


def down_grad(weights, drops, plan, cots, after=()):
    size, width = drops[0].shape
    feat = cots[0].shape[-1]
    tile = 256 if width % 256 == 0 else 128
    tokens = len(plan) * size
    return pl.pallas_call(
        functools.partial(down_grad_kernel, plan, len(drops)),
        out_shape=jax.ShapeDtypeStruct((width, feat), bf16),
        grid=(width // tile,),
        in_specs=[pl.BlockSpec((len(plan), size, 1), lambda i: (0, 0, 0))]
        + [ANY] * (len(drops) + len(cots) + len(after)),
        out_specs=pl.BlockSpec((tile, feat), lambda i: (i, 0)),
        scratch_shapes=[
            pltpu.VMEM((len(plan), size, width), bf16),
            pltpu.VMEM((CHUNKS,) + cots[0].shape, bf16),
            pltpu.SemaphoreType.DMA((len(plan) + CHUNKS,)),
        ],
        compiler_params=pltpu.CompilerParams(vmem_limit_bytes=VMEM),
        cost_estimate=cost(
            flops=2 * tokens * width * feat,
            bytes_accessed=2 * (tokens * feat + tokens * width + width * feat),
            transcendentals=0,
        ),
    )(weights, *drops, *cots, *after)


def per_device(
    stream_in, grad_out, gate_pre, up_pre, keep_mask, segment_ids, norm_gain, w_gate, w_up, w_down
):
    n_row = lax.axis_size("row")
    n_col = lax.axis_size("col")
    nz = n_col // 2
    tok_col, feat = stream_in.shape
    tok_row, width = gate_pre.shape
    total = tok_col * n_col
    sub = tok_col // CHUNKS
    col, row = lax.axis_index("col"), lax.axis_index("row")
    core, chip = lax.rem(col, 2), lax.div(col, 2)
    ring = [0] + list(range(1, nz, 2)) + list(range(nz - 2 + nz % 2, 0, -2))
    after_of = {ring[i]: ring[(i + 1) % nz] for i in range(nz)}

    def spots(chips):
        return jnp.stack([core] + [lax.bitwise_xor(c, row) for c in chips]).astype(jnp.int32)

    held = [sum(jnp.where(chip == ring[p], ring[(p - s) % nz], 0) for p in range(nz)) for s in range(nz)]
    around = spots(held)
    along = spots(range(nz))
    z_groups = [[2 * z + c for z in range(nz)] for c in range(2)]

    def swap(a):
        return lax.ppermute(a, "col", [(i, i ^ 1) for i in range(n_col)])

    def z_exchange(a):
        return lax.all_to_all(
            a, "col", split_axis=0, concat_axis=0, axis_index_groups=z_groups, tiled=True
        )

    def z_next(a):
        return lax.ppermute(a, "col", [(i, 2 * after_of[i // 2] + i % 2) for i in range(n_col)])

    def row_step(a, j):
        return lax.ppermute(a, "row", [(i, i ^ j) for i in range(n_row)])

    def near(a):
        return {j: row_step(a, j) for j in [1] + list(range(2, n_row, 2))}

    def far(got):
        return {k + 1: (row_step(a, k), row_step(b, 1)) for k, (a, b) in got.items()}

    def to_pass(got, after=()):
        first = pick(got[1], 0, after)
        return {k: (first, pick(got[k], 1, after)) for k in range(2, n_row, 2)}

    def all_slots(own, near_ones, far_ones):
        return [own] + list(near_ones.values()) + [a for two in far_ones.values() for a in two]

    nears, fars = [0, 1] + list(range(2, n_row, 2)), list(range(3, n_row, 2))

    def plan_of(half, base=0):
        return [
            (base + nears.index(j), half)
            if j in nears
            else (base + len(nears) + 2 * fars.index(j) + half, None)
            for j in range(n_row)
        ]

    def row_total(a):
        j = 1
        while j < n_row:
            a = a + row_step(a, j)
            j = 2 * j
        return a

    gate, up, keep = (a.reshape(2, CHUNKS, sub, width) for a in (gate_pre, up_pre, keep_mask))
    drop = masked(gate, up, keep)
    assert CHUNKS == 2
    drop_near = [near(a) for a in drop]
    drop_far = far({k: (drop_near[0][1], drop_near[1][k]) for k in range(2, n_row, 2)})
    drop_slots = [
        [drop[h]]
        + [drop_near[h][j] if j in drop_near[h] else drop_far[j][h] for j in range(1, n_row)]
        for h in range(CHUNKS)
    ]
    drops = drop_slots[0] + drop_slots[1]
    far_ones = [a for two in drop_far.values() for a in two]

    xs = stream_in.astype(f32)
    left_over = jnp.sum(xs * xs, axis=1)
    rows = [segment_ids.astype(f32)]
    for _ in range(3):
        rows.append(lax.reduce_precision(left_over, 8, 7))
        left_over = left_over - rows[-1]
    note = jnp.stack([jnp.pad(a, (0, width - a.shape[0])) for a in rows]).astype(bf16)
    note = jnp.pad(note, ((0, 12), (0, 0)))
    gain = norm_gain.reshape(1, feat)

    def read(notes):
        notes = jnp.stack([a[:4].astype(f32) for a in notes])
        onehot = (notes[:, 0, :tok_row, None] == jnp.arange(SEGS, dtype=f32)).astype(f32)
        counts = jnp.sum(onehot, axis=(0, 1))
        weights = jnp.sum(onehot * (total / (SEGS * counts)), axis=2)
        squares = jnp.sum(notes[:, 3, :tok_col] + notes[:, 2, :tok_col] + notes[:, 1, :tok_col], axis=0)
        recip = lax.rsqrt(squares / D + eps)
        return weights.reshape(n_row, 2, CHUNKS, sub), recip[:, None]

    def cot_gather(k, after):
        if k == 0:
            slots = [take(grad_out, 0, sub, 1, [drop[0]])[0]]
            for s in range(1, nz):
                slots.append(z_next(slots[-1]))
            return around, join(
                slots, [a for got in drop_near + [dict(enumerate(far_ones))] for a in got.values()]
            )
        return along, z_exchange(take(grad_out, k, sub, nz, after))

    cots, hids, hid_near, pairs, settled, slots = [], [], [], [], [], []
    plans = [[], []]
    plan = plan_of(0) + plan_of(1)

    def multiply(k, passed, after):
        mine = all_slots(hids[k], hid_near[k], far(passed))
        give, rest = hidden(along, mine, plan, w_gate, w_up, nz, after)
        for h in range(2):
            plans[h].extend(plan_of(h, len(slots)))
        slots.extend(mine)
        pairs.append(add_pair(rest, swap(give)))
        return give

    for k in range(CHUNKS):
        if k == 0:
            where, mine = cot_gather(0, [])
            other = swap(mine)
            late = []
        else:
            where, mine = along, z_exchange(take(grad_out, k, sub, nz, [other]))
            mine = hold(mine, [hids[-1]])
            other = swap(mine)
            late = [normed] if k == 1 else []
        cot, *partial = back(where, mine, other, w_down, [] if k else [note], late)
        cots.append(cot)
        parts = [partial[0]] + [row_step(partial[j], j) for j in range(1, n_row)]
        if k == 0:
            every, recip = read([a[2 * sub :] for a in parts])
            weights = every[0][:, :, :, None]
            all_weights = every.transpose(2, 0, 1, 3).reshape(CHUNKS * n_row, 2 * sub, 1)
            late = []
        else:
            late = [multiply(k - 1, to_pass(hid_near[-1], [partial[0]]), pairs[-1:])]
        hids.append(hidden_grads(k, parts, gate, up, keep, weights, late))
        hid_near.append(near(hids[k]))
        if k == 0:
            normed = normalize(stream_in, recip, gain, nz, [hids[0]])
            normed_mine = z_exchange(normed)
    order = [(i, None) for i in range(len(drops))]
    grad_down = down_grad(all_weights, drops, order, cots, [hids[-1]])
    multiply(CHUNKS - 1, to_pass(hid_near[-1], [grad_down]), pairs[-1:])
    normed_other = swap(normed_mine)
    for k in range(CHUNKS):
        late = []
        if k == CHUNKS - 1:
            grad_gate, grad_up = weight_grads(
                along,
                normed_mine,
                normed_other,
                slots,
                plans[0] + plans[1],
                pairs[-1:] + [s[1] for s in settled],
            )
            late = [grad_gate]
        settled.append(settle(k, z_exchange(pairs[k]), gain, stream_in, late))
    scaled = jnp.concatenate([s[0] for s in settled], axis=0)
    inner = jnp.concatenate([s[1] for s in settled], axis=0)
    inner = inner + sum(row_step(inner, j) for j in range(1, n_row))
    inner = inner[:, :1] / D
    branch = recip * (scaled - xs * (recip * recip * inner))
    grad_in = (grad_out.astype(f32) + branch).astype(bf16)
    return (grad_in, grad_gate, grad_up, grad_down)


def solution(mesh):
    return jax.shard_map(
        per_device,
        mesh=mesh,
        in_specs=(
            P("col", "row"),
            P("col", "row"),
            P("row", "col"),
            P("row", "col"),
            P("row", "col"),
            P("row"),
            P("row"),
            P("row", "col"),
            P("row", "col"),
            P("col", "row"),
        ),
        out_specs=(P("col", "row"), P("row", "col"), P("row", "col"), P("col", "row")),
        check_vma=False,
    )
```

time: 302 us -> 268 us (0.89)
  Pallas kernels: 59.8 us -> 126 us
  matrix products: 32.4 us -> 0 us
  waiting for transfers between devices: 99.7 us -> 71.7 us
  local copies, waits for them, and re-layouts: 35.9 us -> 14.5 us
  starting transfers between devices: 63.4 us -> 49.5 us
  other arithmetic: 8.11 us -> 3.44 us
    pallas_call x4 -> x17, Pallas kernels: 32.6 us -> 97.3 us  [the longest x2 28.2 us: hidden(): pl.pallas_call(functools.partial(hidden_kernel, n, plan, len(slots)), out...]
    ppermute x12 -> x0, waiting for transfers between devices: 48.4 us -> none  [z_step(): return lax.ppermute(a, 'col', [(i, i ^ 2 * s) for i in range(n_col)])]
    dot_general x3 -> x0, matrix products: 32.4 us -> none  [over_tokens(): lax.dot_general(left, right, (((0,), (0,)), ((), ())), preferred_element_...]
    ppermute x12 -> x0, starting transfers between devices: 26.2 us -> none  [z_step(): return lax.ppermute(a, 'col', [(i, i ^ 2 * s) for i in range(n_col)])]
    all_to_all x0 -> x4, starting transfers between devices: none -> 18.1 us  [z_exchange(): lax.all_to_all(a, 'col', split_axis=0, concat_axis=0, axis_index_groups=z...]
    ppermute x24 -> x23, waiting for transfers between devices: 41.1 us -> 55.1 us  [row_step(): return lax.ppermute(a, 'row', [(i, i ^ j) for i in range(n_row)])]
    unnamed x83 -> x60, local copies, waits for them, and re-layouts: 21.3 us -> 8.31 us
    squeeze x12 -> x0, local copies, waits for them, and re-layouts: 8.27 us -> none  [the longest x8 6 us: row_far(): halves = {j: (got[j][0], got[j][1]) for j in got}]
  transfers between devices with their start and end apart: 44 -> 35, of which waited for: 12 -> 21; matrix products, arithmetic and copies ran while one was open for 21% -> 3% of each run, Pallas kernels for 20% -> 41%
where the time goes in v2:
time: 268 us; the launch traced here: 266 us
  Pallas kernels  126 us (47%)
  waiting for transfers between devices  71.7 us (27%)
  starting transfers between devices  49.5 us (18%)
  local copies, waits for them, and re-layouts  14.5 us (5%)
  other arithmetic  3.44 us (1%)
    ppermute x23, waiting for transfers between devices, row_step(): return lax.ppermute(a, 'row', [(i, i ^ j) for i in range(n_row)])  55.1 us
    pallas_call x2, Pallas kernels, hidden(): pl.pallas_call(functools.partial(hidden_kernel, n, plan, len(slots)), out...  28.2 us
    ppermute x23, starting transfers between devices, row_step(): return lax.ppermute(a, 'row', [(i, i ^ j) for i in range(n_row)])  27.4 us
    pallas_call x1, Pallas kernels, weight_grads(): pl.pallas_call(functools.partial(weight_grads_kernel, n, plan, len(slots)...  22.6 us
    pallas_call x2, Pallas kernels, back(): pl.pallas_call(functools.partial(back_kernel, n), out_shape=(jax.ShapeDty...  19.2 us
    all_to_all x4, starting transfers between devices, z_exchange(): lax.all_to_all(a, 'col', split_axis=0, concat_axis=0, axis_index_groups=z...  18.1 us
    pallas_call x1, Pallas kernels, down_grad(): pl.pallas_call(functools.partial(down_grad_kernel, plan, len(drops)), out...  16.8 us
    ppermute x3, waiting for transfers between devices, z_next(): lax.ppermute(a, 'col', [(i, 2 * after_of[i // 2] + i % 2) for i in range(...  9.52 us
  transfers between devices with their start and end apart: 35, of which 21 were waited for; matrix products, arithmetic and copies ran while one was open for 3% of the time, Pallas kernels for 41%

profile of v2, /device:TPU:0, one launch (start us, length us, event | category | flops | bytes accessed | tf_op | source)
XLA Modules:
  0.0 266.4 jit_solution(14388475580165656598)
XLA Ops:
  0.6 3.0 %shard_map.129 = (bf16[128,1792]{1,0:T(8,128)(2,1)}, bf16[128,1792]{1,0:T(8,128)(2,1)}) custom-call(bf16[2,2,64,1792]{3,2,1,0:T(8,128)(2,1)} %bitcast.31, bf16[2,2,64,1792]{3,2,1,0:T(8,128)(2,1)} %bitcast.34, s32[2,2,64,1792]{3,2,1,0:T(8,128)} %bitcast.28), custom_call_target="tpu_custom_call" | custom-call | flops 573440 | bytes 573440 | tf_op jit(solution)/shard_map/pallas_call | solution.py:327
  3.7 2.9 %collective-permute-start.3 = (bf16[128,1792]{1,0:T(8,128)(2,1)}, bf16[128,1792]{1,0:T(8,128)(2,1)S(1)}, u32[]{:S(2)}, u32[]{:S(2)}) collective-permute-start(bf16[128,1792]{1,0:T(8,128)(2,1)} %get-tuple-element.26.refs_0_), channel_id=1, source_target_pairs={{0,8},{8,0},{16,24},{24,16},{1,9},{9,1},{17,25},{25,17},{2,10},{10... | collective-permute-start | bytes 1376264 | tf_op jit(solution)/shard_map/ppermute | solution.py:518
  11.4 7.0 %collective-permute-done.refs_1_ = bf16[64,2048]{1,0:T(8,128)(2,1)S(1)} collective-permute-done((bf16[64,2048]{1,0:T(8,128)(2,1)}, bf16[64,2048]{1,0:T(8,128)(2,1)S(1)}, u32[]{:S(2)}, u32[]{:S(2)}) %collective-permute-start) | collective-permute-done | bytes 262176 | tf_op jit(solution)/shard_map/ppermute | solution.py:515
  23.4 2.5 collective-permute-done.1.refs_2_
  26.7 6.3 %collective-permute-done.4.refs_5_.refs_2_ = bf16[128,1792]{1,0:T(8,128)(2,1)S(1)} collective-permute-done((bf16[128,1792]{1,0:T(8,128)(2,1)}, bf16[128,1792]{1,0:T(8,128)(2,1)S(1)}, u32[]{:S(2)}, u32[]{:S(2)}) %collective-permute-start.4) | collective-permute-done | bytes 458784 | tf_op jit(solution)/shard_map/ppermute | solution.py:518
  33.5 6.4 %collective-permute-done.7.refs_8_.refs_3_ = bf16[128,1792]{1,0:T(8,128)(2,1)S(1)} collective-permute-done((bf16[128,1792]{1,0:T(8,128)(2,1)S(1)}, bf16[128,1792]{1,0:T(8,128)(2,1)S(1)}, u32[]{:S(2)}, u32[]{:S(2)}) %collective-permute-start.7) | collective-permute-done | bytes 458784 | tf_op jit(solution)/shard_map/ppermute | solution.py:518
  41.4 2.2 shard_map.131.mine
  47.5 9.7 %shard_map.132 = (bf16[4,2,64,2048]{3,2,1,0:T(8,128)(2,1)}, bf16[144,1792]{1,0:T(8,128)(2,1)}, bf16[144,1792]{1,0:T(8,128)(2,1)}, bf16[144,1792]{1,0:T(8,128)(2,1)}, bf16[144,1792]{1,0:T(8,128)(2,1)}) custom-call(s32[5]{0:T(128)} %stack.81.where, bf16[4,64,2048]{2,1,0:T(8,128)(2,1)} %shard_map.131.mine, bf16[4,64,2048]{2,1,0:T(8,128)(2,1)} %copy-done.7, ...), custom_call_target="tpu_custom_call" | custom-call | flops 469762048 | bytes 1671168 | tf_op jit(solution)/shard_map/pallas_call | solution.py:287
  63.5 4.5 %all-to-all-start = ((bf16[4,64,2048]{2,1,0:T(8,128)(2,1)}), bf16[4,64,2048]{2,1,0:T(8,128)(2,1)S(1)}, u32[]{:S(2)}, u32[]{:S(2)}) async-start(bf16[4,64,2048]{2,1,0:T(8,128)(2,1)} %shard_map.134), calls=%async_computation | async-start | bytes 2097152 | tf_op jit(solution)/shard_map/all_to_all | solution.py:510
  68.0 4.9 %collective-permute-done.12.refs_3_ = bf16[144,1792]{1,0:T(8,128)(2,1)S(1)} collective-permute-done((bf16[144,1792]{1,0:T(8,128)(2,1)}, bf16[144,1792]{1,0:T(8,128)(2,1)S(1)}, u32[]{:S(2)}, u32[]{:S(2)}) %collective-permute-start.12) | collective-permute-done | bytes 516128 | tf_op jit(solution)/shard_map/ppermute | solution.py:518
  73.0 10.0 %collective-permute-done.11.refs_2_ = bf16[144,1792]{1,0:T(8,128)(2,1)S(1)} collective-permute-done((bf16[144,1792]{1,0:T(8,128)(2,1)}, bf16[144,1792]{1,0:T(8,128)(2,1)S(1)}, u32[]{:S(2)}, u32[]{:S(2)}) %collective-permute-start.11) | collective-permute-done | bytes 516128 | tf_op jit(solution)/shard_map/ppermute | solution.py:518
  85.1 3.8 %shard_map.133.refs_0_ = bf16[2,128,1792]{2,1,0:T(8,128)(2,1)} custom-call(bf16[144,1792]{1,0:T(8,128)(2,1)} %get-tuple-element.28.refs_0_, bf16[144,1792]{1,0:T(8,128)(2,1)} %copy-done.21, bf16[144,1792]{1,0:T(8,128)(2,1)} %copy-done.20, bf16[144,1792]{1,0:T(8,128)(2,1)} %copy-done.19, bf16[2,2,64,1792]{3,2,1,0:T(8,128)(2,1)} %bitcast.32, ...), custom_call_target="tpu_custom_call" | custom-call | flops 573440 | bytes 573440 | tf_op jit(solution)/shard_map/pallas_call | solution.py:363
  88.9 2.6 shard_map.136.refs_0_
  94.2 3.8 %all-to-all-start.3 = ((bf16[4,128,2048]{2,1,0:T(8,128)(2,1)}), bf16[4,128,2048]{2,1,0:T(8,128)(2,1)S(1)}, u32[]{:S(2)}, u32[]{:S(2)}) async-start(bf16[4,128,2048]{2,1,0:T(8,128)(2,1)} %shard_map.136.refs_0_), calls=%async_computation.3 | async-start | bytes 4194304 | tf_op jit(solution)/shard_map/all_to_all | solution.py:510
  98.0 2.4 shard_map.135.mine
  103.4 9.6 %shard_map.137 = (bf16[4,2,64,2048]{3,2,1,0:T(8,128)(2,1)}, bf16[128,1792]{1,0:T(8,128)(2,1)}, bf16[128,1792]{1,0:T(8,128)(2,1)}, bf16[128,1792]{1,0:T(8,128)(2,1)}, bf16[128,1792]{1,0:T(8,128)(2,1)}) custom-call(s32[5]{0:T(128)} %stack.97.where, bf16[4,64,2048]{2,1,0:T(8,128)(2,1)} %shard_map.135.mine, bf16[4,64,2048]{2,1,0:T(8,128)(2,1)} %collective-permute-done.15.other, ...), custom_call_target="tpu_custom_call" | custom-call | flops 469762048 | bytes 1671168 | tf_op jit(solution)/shard_map/pallas_call | solution.py:287
  113.0 10.3 %collective-permute-done.14.a_ref.refs_2_ = bf16[2,128,1792]{2,1,0:T(8,128)(2,1)} collective-permute-done((bf16[2,128,1792]{2,1,0:T(8,128)(2,1)S(1)}, bf16[2,128,1792]{2,1,0:T(8,128)(2,1)}, u32[]{:S(2)}, u32[]{:S(2)}) %collective-permute-start.14) | collective-permute-done | bytes 917536 | tf_op jit(solution)/shard_map/ppermute | solution.py:518
  131.9 6.8 %collective-permute-done.17.refs_4_ = bf16[128,1792]{1,0:T(8,128)(2,1)S(1)} collective-permute-done((bf16[128,1792]{1,0:T(8,128)(2,1)}, bf16[128,1792]{1,0:T(8,128)(2,1)S(1)}, u32[]{:S(2)}, u32[]{:S(2)}) %collective-permute-start.17) | collective-permute-done | bytes 458784 | tf_op jit(solution)/shard_map/ppermute | solution.py:518
  138.7 2.4 collective-permute-done.16.refs_3_
  141.9 14.1 %shard_map.140 = (bf16[4,64,2048]{2,1,0:T(8,128)(2,1)}, f32[4,64,2048]{2,1,0:T(8,128)}) custom-call(s32[5]{0:T(128)} %stack.97.where, bf16[2,128,1792]{2,1,0:T(8,128)(2,1)} %shard_map.133.refs_0_, bf16[2,128,1792]{2,1,0:T(8,128)(2,1)} %collective-permute-done.13.a_ref.refs_1_, bf16[2,128,1792]{2,1,0:T(8,128)(2,1)} %collective-permute-done.14.a_ref.refs_2_, ...), custom_call_target="tpu_custom_call" | custom-call | flops 939524096 | bytes 2686976 | tf_op jit(solution)/shard_map/pallas_call | solution.py:411
  156.1 3.1 %collective-permute-done.20.refs_2_ = bf16[128,1792]{1,0:T(8,128)(2,1)S(1)} collective-permute-done((bf16[128,1792]{1,0:T(8,128)(2,1)}, bf16[128,1792]{1,0:T(8,128)(2,1)S(1)}, u32[]{:S(2)}, u32[]{:S(2)}) %collective-permute-start.20) | collective-permute-done | bytes 458784 | tf_op jit(solution)/shard_map/ppermute | solution.py:518
  160.0 3.7 %shard_map.143.refs_10_.refs_0_.refs_5_ = bf16[2,128,1792]{2,1,0:T(8,128)(2,1)} custom-call(bf16[128,1792]{1,0:T(8,128)(2,1)} %get-tuple-element.32.refs_0_, bf16[128,1792]{1,0:T(8,128)(2,1)} %copy-done.23, bf16[128,1792]{1,0:T(8,128)(2,1)} %copy-done.24, bf16[128,1792]{1,0:T(8,128)(2,1)} %collective-permute-done.21.refs_3_, ...), custom_call_target="tpu_custom_call" | custom-call | flops 573440 | bytes 573440 | tf_op jit(solution)/shard_map/pallas_call | solution.py:363
  167.6 16.8 %shard_map.144.refs_0_ = bf16[1792,2048]{1,0:T(8,128)(2,1)} custom-call(f32[8,128,1]{2,1,0:T(8,128)} %reshape.67.weight_ref, bf16[128,1792]{1,0:T(8,128)(2,1)} %get-tuple-element.26.refs_0_, bf16[128,1792]{1,0:T(8,128)(2,1)} %copy-done.8, bf16[128,1792]{1,0:T(8,128)(2,1)} %copy-done.10, bf16[128,1792]{1,0:T(8,128)(2,1)} %copy-done.12, ...), custom_call_target="tpu_custom_call" | custom-call | flops 939524096 | bytes 1900544 | tf_op jit(solution)/shard_map/pallas_call | solution.py:462
  191.8 3.0 %shard_map.141.refs_7_ = bf16[4,64,2048]{2,1,0:T(8,128)(2,1)} custom-call(f32[4,64,2048]{2,1,0:T(8,128)} %get-tuple-element.33.rest_ref, bf16[4,64,2048]{2,1,0:T(8,128)(2,1)} %collective-permute-done.18.got_ref), custom_call_target="tpu_custom_call" | custom-call | flops 65536 | bytes 524288 | tf_op jit(solution)/shard_map/pallas_call | solution.py:165
  194.8 4.9 %all-to-all-start.1 = ((bf16[4,64,2048]{2,1,0:T(8,128)(2,1)}), bf16[4,64,2048]{2,1,0:T(8,128)(2,1)}, u32[]{:S(2)}, u32[]{:S(2)}) async-start(bf16[4,64,2048]{2,1,0:T(8,128)(2,1)} %shard_map.141.refs_7_), calls=%async_computation.1 | async-start | bytes 2097152 | tf_op jit(solution)/shard_map/all_to_all | solution.py:510
  201.6 14.0 %shard_map.147 = (bf16[4,64,2048]{2,1,0:T(8,128)(2,1)}, f32[4,64,2048]{2,1,0:T(8,128)}) custom-call(s32[5]{0:T(128)} %stack.97.where, bf16[2,128,1792]{2,1,0:T(8,128)(2,1)} %shard_map.143.refs_10_.refs_0_.refs_5_, bf16[2,128,1792]{2,1,0:T(8,128)(2,1)} %collective-permute-done.22.a_ref.refs_1_.refs_6_, bf16[2,128,1792]{2,1,0:T(8,128)(2,1)} %copy-done.4, ...), custom_call_target="tpu_custom_call" | custom-call | flops 939524096 | bytes 2686976 | tf_op jit(solution)/shard_map/pallas_call | solution.py:411
  216.2 3.0 %collective-permute-done.26.got_ref = bf16[4,64,2048]{2,1,0:T(8,128)(2,1)S(1)} collective-permute-done((bf16[4,64,2048]{2,1,0:T(8,128)(2,1)}, bf16[4,64,2048]{2,1,0:T(8,128)(2,1)S(1)}, u32[]{:S(2)}, u32[]{:S(2)}) %collective-permute-start.26) | collective-permute-done | bytes 1048608 | tf_op jit(solution)/shard_map/ppermute | solution.py:507
  220.2 3.0 %shard_map.148.refs_10_ = bf16[4,64,2048]{2,1,0:T(8,128)(2,1)} custom-call(f32[4,64,2048]{2,1,0:T(8,128)} %get-tuple-element.41.rest_ref, bf16[4,64,2048]{2,1,0:T(8,128)(2,1)} %copy-done.18), custom_call_target="tpu_custom_call" | custom-call | flops 65536 | bytes 524288 | tf_op jit(solution)/shard_map/pallas_call | solution.py:165
  223.2 4.9 %all-to-all-start.2 = ((bf16[4,64,2048]{2,1,0:T(8,128)(2,1)}), bf16[4,64,2048]{2,1,0:T(8,128)(2,1)}, u32[]{:S(2)}, u32[]{:S(2)}) async-start(bf16[4,64,2048]{2,1,0:T(8,128)(2,1)} %shard_map.148.refs_10_), calls=%async_computation.2 | async-start | bytes 2097152 | tf_op jit(solution)/shard_map/all_to_all | solution.py:510
  228.1 2.3 shard_map.142
  231.1 22.6 %shard_map.149 = (bf16[2048,1792]{1,0:T(8,128)(2,1)}, bf16[2048,1792]{1,0:T(8,128)(2,1)}) custom-call(s32[5]{0:T(128)} %stack.97.where, bf16[4,128,2048]{2,1,0:T(8,128)(2,1)} %copy-done.3, bf16[4,128,2048]{2,1,0:T(8,128)(2,1)} %collective-permute-done.27.other, bf16[2,128,1792]{2,1,0:T(8,128)(2,1)} %shard_map.133.refs_0_, ...), custom_call_target="tpu_custom_call" | custom-call | flops 1879048192 | bytes 3276800 | tf_op jit(solution)/shard_map/pallas_call | solution.py:245
  254.2 2.4 shard_map.150
  (154 shorter events, 66.5 us)
Async XLA Ops:
  3.7 16.7 %collective-permute-start.3 = (bf16[128,1792]{1,0:T(8,128)(2,1)}, bf16[128,1792]{1,0:T(8,128)(2,1)S(1)}, u32[]{:S(2)}, u32[]{:S(2)}) collective-permute-start(bf16[128,1792]{1,0:T(8,128)(2,1)} %get-tuple-element.26.refs_0_), channel_id=1, source_target_pairs={{0,8},{8,0},{16,24},{24,16},{1,9},{9,1},{17,25},{25,17},{2,10},{10... | collective-permute-start | bytes 1376264 | tf_op jit(solution)/shard_map/ppermute | solution.py:518
  6.6 15.3 %collective-permute-start.6 = (bf16[128,1792]{1,0:T(8,128)(2,1)}, bf16[128,1792]{1,0:T(8,128)(2,1)S(1)}, u32[]{:S(2)}, u32[]{:S(2)}) collective-permute-start(bf16[128,1792]{1,0:T(8,128)(2,1)} %get-tuple-element.27.refs_4_), channel_id=1, source_target_pairs={{0,16},{8,24},{16,0},{24,8},{1,17},{9,25},{17,1},{25,9},{2,18},{10... | collective-permute-start | bytes 1376264 | tf_op jit(solution)/shard_map/ppermute | solution.py:518
  9.8 8.6 %collective-permute-start = (bf16[64,2048]{1,0:T(8,128)(2,1)}, bf16[64,2048]{1,0:T(8,128)(2,1)S(1)}, u32[]{:S(2)}, u32[]{:S(2)}) collective-permute-start(bf16[64,2048]{1,0:T(8,128)(2,1)} %bitcast.37), channel_id=1, source_target_pairs={{0,2},{1,3},{2,6},{3,7},{4,0},{5,1},{6,4},{7,5},{8,10},{9,11},{10,... | collective-permute-start | bytes 786440 | tf_op jit(solution)/shard_map/ppermute | solution.py:515
  18.4 7.5 %collective-permute-start.1 = (bf16[64,2048]{1,0:T(8,128)(2,1)S(1)}, bf16[64,2048]{1,0:T(8,128)(2,1)S(1)}, u32[]{:S(2)}, u32[]{:S(2)}) collective-permute-start(bf16[64,2048]{1,0:T(8,128)(2,1)S(1)} %collective-permute-done.refs_1_), channel_id=1, source_target_pairs={{0,2},{1,3},{2,6},{3,7},{4,0},{5,1},{6,4},{7,5},{8,10},{9,11},{10,... | collective-permute-start | bytes 786440 | tf_op jit(solution)/shard_map/ppermute | solution.py:515
  19.3 13.7 %collective-permute-start.4 = (bf16[128,1792]{1,0:T(8,128)(2,1)}, bf16[128,1792]{1,0:T(8,128)(2,1)S(1)}, u32[]{:S(2)}, u32[]{:S(2)}) collective-permute-start(bf16[128,1792]{1,0:T(8,128)(2,1)} %get-tuple-element.26.refs_0_), channel_id=1, source_target_pairs={{0,16},{8,24},{16,0},{24,8},{1,17},{9,25},{17,1},{25,9},{2,18},{10... | collective-permute-start | bytes 1376264 | tf_op jit(solution)/shard_map/ppermute | solution.py:518
  19.8 13.7 %collective-permute-start.5 = (bf16[128,1792]{1,0:T(8,128)(2,1)}, bf16[128,1792]{1,0:T(8,128)(2,1)S(1)}, u32[]{:S(2)}, u32[]{:S(2)}) collective-permute-start(bf16[128,1792]{1,0:T(8,128)(2,1)} %get-tuple-element.27.refs_4_), channel_id=1, source_target_pairs={{0,8},{8,0},{16,24},{24,16},{1,9},{9,1},{17,25},{25,17},{2,10},{10... | collective-permute-start | bytes 1376264 | tf_op jit(solution)/shard_map/ppermute | solution.py:518
  20.3 19.5 %collective-permute-start.7 = (bf16[128,1792]{1,0:T(8,128)(2,1)S(1)}, bf16[128,1792]{1,0:T(8,128)(2,1)S(1)}, u32[]{:S(2)}, u32[]{:S(2)}) collective-permute-start(bf16[128,1792]{1,0:T(8,128)(2,1)S(1)} %collective-permute-done.3.refs_4_.refs_1_), channel_id=1, source_target_pairs={{0,16},{8,24},{16,0},{24,8},{1,17},{9,25},{17,1},{25,9},{2,18},{10... | collective-permute-start | bytes 1376264 | tf_op jit(solution)/shard_map/ppermute | solution.py:518
  21.9 18.2 %collective-permute-start.8 = (bf16[128,1792]{1,0:T(8,128)(2,1)S(1)}, bf16[128,1792]{1,0:T(8,128)(2,1)S(1)}, u32[]{:S(2)}, u32[]{:S(2)}) collective-permute-start(bf16[128,1792]{1,0:T(8,128)(2,1)S(1)} %collective-permute-done.6.refs_7_.refs_6_), channel_id=1, source_target_pairs={{0,8},{8,0},{16,24},{24,16},{1,9},{9,1},{17,25},{25,17},{2,10},{10... | collective-permute-start | bytes 1376264 | tf_op jit(solution)/shard_map/ppermute | solution.py:518
  25.9 7.6 %collective-permute-start.2 = (bf16[64,2048]{1,0:T(8,128)(2,1)S(1)}, bf16[64,2048]{1,0:T(8,128)(2,1)S(1)}, u32[]{:S(2)}, u32[]{:S(2)}) collective-permute-start(bf16[64,2048]{1,0:T(8,128)(2,1)S(1)} %collective-permute-done.1.refs_2_), channel_id=1, source_target_pairs={{0,2},{1,3},{2,6},{3,7},{4,0},{5,1},{6,4},{7,5},{8,10},{9,11},{10,... | collective-permute-start | bytes 786440 | tf_op jit(solution)/shard_map/ppermute | solution.py:515
  57.2 15.8 %collective-permute-start.12 = (bf16[144,1792]{1,0:T(8,128)(2,1)}, bf16[144,1792]{1,0:T(8,128)(2,1)S(1)}, u32[]{:S(2)}, u32[]{:S(2)}) collective-permute-start(bf16[144,1792]{1,0:T(8,128)(2,1)} %get-tuple-element.31), channel_id=1, source_target_pairs={{0,24},{8,16},{16,8},{24,0},{1,25},{9,17},{17,9},{25,1},{2,26},{10... | collective-permute-start | bytes 1548296 | tf_op jit(solution)/shard_map/ppermute | solution.py:518
  58.2 24.8 %collective-permute-start.11 = (bf16[144,1792]{1,0:T(8,128)(2,1)}, bf16[144,1792]{1,0:T(8,128)(2,1)S(1)}, u32[]{:S(2)}, u32[]{:S(2)}) collective-permute-start(bf16[144,1792]{1,0:T(8,128)(2,1)} %get-tuple-element.30), channel_id=1, source_target_pairs={{0,16},{8,24},{16,0},{24,8},{1,17},{9,25},{17,1},{25,9},{2,18},{10... | collective-permute-start | bytes 1548296 | tf_op jit(solution)/shard_map/ppermute | solution.py:518
  59.2 23.8 %collective-permute-start.10 = (bf16[144,1792]{1,0:T(8,128)(2,1)}, bf16[144,1792]{1,0:T(8,128)(2,1)S(1)}, u32[]{:S(2)}, u32[]{:S(2)}) collective-permute-start(bf16[144,1792]{1,0:T(8,128)(2,1)} %get-tuple-element.29), channel_id=1, source_target_pairs={{0,8},{8,0},{16,24},{24,16},{1,9},{9,1},{17,25},{25,17},{2,10},{10... | collective-permute-start | bytes 1548296 | tf_op jit(solution)/shard_map/ppermute | solution.py:518
  63.5 29.7 %all-to-all-start = ((bf16[4,64,2048]{2,1,0:T(8,128)(2,1)}), bf16[4,64,2048]{2,1,0:T(8,128)(2,1)S(1)}, u32[]{:S(2)}, u32[]{:S(2)}) async-start(bf16[4,64,2048]{2,1,0:T(8,128)(2,1)} %shard_map.134), calls=%async_computation | async-start | bytes 2097152 | tf_op jit(solution)/shard_map/all_to_all | solution.py:510
  94.2 100.6 %all-to-all-start.3 = ((bf16[4,128,2048]{2,1,0:T(8,128)(2,1)}), bf16[4,128,2048]{2,1,0:T(8,128)(2,1)S(1)}, u32[]{:S(2)}, u32[]{:S(2)}) async-start(bf16[4,128,2048]{2,1,0:T(8,128)(2,1)} %shard_map.136.refs_0_), calls=%async_computation.3 | async-start | bytes 4194304 | tf_op jit(solution)/shard_map/all_to_all | solution.py:510
  100.4 22.9 %collective-permute-start.14 = (bf16[2,128,1792]{2,1,0:T(8,128)(2,1)S(1)}, bf16[2,128,1792]{2,1,0:T(8,128)(2,1)}, u32[]{:S(2)}, u32[]{:S(2)}) collective-permute-start(bf16[2,128,1792]{2,1,0:T(8,128)(2,1)S(1)} %copy-done), channel_id=1, source_target_pairs={{0,16},{8,24},{16,0},{24,8},{1,17},{9,25},{17,1},{25,9},{2,18},{10... | collective-permute-start | bytes 2752520 | tf_op jit(solution)/shard_map/ppermute | solution.py:518
  101.4 24.2 %collective-permute-start.13 = (bf16[2,128,1792]{2,1,0:T(8,128)(2,1)S(1)}, bf16[2,128,1792]{2,1,0:T(8,128)(2,1)}, u32[]{:S(2)}, u32[]{:S(2)}) collective-permute-start(bf16[2,128,1792]{2,1,0:T(8,128)(2,1)S(1)} %copy-done), channel_id=1, source_target_pairs={{0,8},{8,0},{16,24},{24,16},{1,9},{9,1},{17,25},{25,17},{2,10},{10... | collective-permute-start | bytes 2752520 | tf_op jit(solution)/shard_map/ppermute | solution.py:518
  125.1 13.6 %collective-permute-start.17 = (bf16[128,1792]{1,0:T(8,128)(2,1)}, bf16[128,1792]{1,0:T(8,128)(2,1)S(1)}, u32[]{:S(2)}, u32[]{:S(2)}) collective-permute-start(bf16[128,1792]{1,0:T(8,128)(2,1)} %shard_map.139), channel_id=1, source_target_pairs={{0,8},{8,0},{16,24},{24,16},{1,9},{9,1},{17,25},{25,17},{2,10},{10... | collective-permute-start | bytes 1376264 | tf_op jit(solution)/shard_map/ppermute | solution.py:518
  127.4 13.7 %collective-permute-start.16 = (bf16[128,1792]{1,0:T(8,128)(2,1)}, bf16[128,1792]{1,0:T(8,128)(2,1)S(1)}, u32[]{:S(2)}, u32[]{:S(2)}) collective-permute-start(bf16[128,1792]{1,0:T(8,128)(2,1)} %shard_map.138), channel_id=1, source_target_pairs={{0,16},{8,24},{16,0},{24,8},{1,17},{9,25},{17,1},{25,9},{2,18},{10... | collective-permute-start | bytes 1376264 | tf_op jit(solution)/shard_map/ppermute | solution.py:518
  128.5 27.7 %collective-permute-start.19 = (bf16[128,1792]{1,0:T(8,128)(2,1)}, bf16[128,1792]{1,0:T(8,128)(2,1)S(1)}, u32[]{:S(2)}, u32[]{:S(2)}) collective-permute-start(bf16[128,1792]{1,0:T(8,128)(2,1)} %get-tuple-element.36), channel_id=1, source_target_pairs={{0,8},{8,0},{16,24},{24,16},{1,9},{9,1},{17,25},{25,17},{2,10},{10... | collective-permute-start | bytes 1376264 | tf_op jit(solution)/shard_map/ppermute | solution.py:518
  129.9 29.2 %collective-permute-start.20 = (bf16[128,1792]{1,0:T(8,128)(2,1)}, bf16[128,1792]{1,0:T(8,128)(2,1)S(1)}, u32[]{:S(2)}, u32[]{:S(2)}) collective-permute-start(bf16[128,1792]{1,0:T(8,128)(2,1)} %get-tuple-element.37), channel_id=1, source_target_pairs={{0,16},{8,24},{16,0},{24,8},{1,17},{9,25},{17,1},{25,9},{2,18},{10... | collective-permute-start | bytes 1376264 | tf_op jit(solution)/shard_map/ppermute | solution.py:518
  131.0 28.2 %collective-permute-start.21 = (bf16[128,1792]{1,0:T(8,128)(2,1)}, bf16[128,1792]{1,0:T(8,128)(2,1)}, u32[]{:S(2)}, u32[]{:S(2)}) collective-permute-start(bf16[128,1792]{1,0:T(8,128)(2,1)} %get-tuple-element.38), channel_id=1, source_target_pairs={{0,24},{8,16},{16,8},{24,0},{1,25},{9,17},{17,9},{25,1},{2,26},{10... | collective-permute-start | bytes 1376264 | tf_op jit(solution)/shard_map/ppermute | solution.py:518
  156.0 35.7 %collective-permute-start.18 = (bf16[4,64,2048]{2,1,0:T(8,128)(2,1)}, bf16[4,64,2048]{2,1,0:T(8,128)(2,1)}, u32[]{:S(2)}, u32[]{:S(2)}) collective-permute-start(bf16[4,64,2048]{2,1,0:T(8,128)(2,1)} %get-tuple-element.34.refs_8_), channel_id=1, source_target_pairs={{0,1},{1,0},{2,3},{3,2},{4,5},{5,4},{6,7},{7,6},{8,9},{9,8},{10,11... | collective-permute-start | bytes 3145736 | tf_op jit(solution)/shard_map/ppermute | solution.py:507
  163.7 20.7 %collective-permute-start.23 = (bf16[2,128,1792]{2,1,0:T(8,128)(2,1)}, bf16[2,128,1792]{2,1,0:T(8,128)(2,1)S(1)}, u32[]{:S(2)}, u32[]{:S(2)}) collective-permute-start(bf16[2,128,1792]{2,1,0:T(8,128)(2,1)} %shard_map.143.refs_10_.refs_0_.refs_5_), channel_id=1, source_target_pairs={{0,16},{8,24},{16,0},{24,8},{1,17},{9,25},{17,1},{25,9},{2,18},{10... | collective-permute-start | bytes 2752520 | tf_op jit(solution)/shard_map/ppermute | solution.py:518
  164.7 24.2 %collective-permute-start.22 = (bf16[2,128,1792]{2,1,0:T(8,128)(2,1)}, bf16[2,128,1792]{2,1,0:T(8,128)(2,1)}, u32[]{:S(2)}, u32[]{:S(2)}) collective-permute-start(bf16[2,128,1792]{2,1,0:T(8,128)(2,1)} %shard_map.143.refs_10_.refs_0_.refs_5_), channel_id=1, source_target_pairs={{0,8},{8,0},{16,24},{24,16},{1,9},{9,1},{17,25},{25,17},{2,10},{10... | collective-permute-start | bytes 2752520 | tf_op jit(solution)/shard_map/ppermute | solution.py:518
  187.1 12.5 %collective-permute-start.25 = (bf16[128,1792]{1,0:T(8,128)(2,1)}, bf16[128,1792]{1,0:T(8,128)(2,1)S(1)}, u32[]{:S(2)}, u32[]{:S(2)}) collective-permute-start(bf16[128,1792]{1,0:T(8,128)(2,1)} %shard_map.146), channel_id=1, source_target_pairs={{0,8},{8,0},{16,24},{24,16},{1,9},{9,1},{17,25},{25,17},{2,10},{10... | collective-permute-start | bytes 1376264 | tf_op jit(solution)/shard_map/ppermute | solution.py:518
  190.7 10.1 %collective-permute-start.24 = (bf16[128,1792]{1,0:T(8,128)(2,1)}, bf16[128,1792]{1,0:T(8,128)(2,1)S(1)}, u32[]{:S(2)}, u32[]{:S(2)}) collective-permute-start(bf16[128,1792]{1,0:T(8,128)(2,1)} %shard_map.145), channel_id=1, source_target_pairs={{0,16},{8,24},{16,0},{24,8},{1,17},{9,25},{17,1},{25,9},{2,18},{10... | collective-permute-start | bytes 1376264 | tf_op jit(solution)/shard_map/ppermute | solution.py:518
  194.8 28.4 %all-to-all-start.1 = ((bf16[4,64,2048]{2,1,0:T(8,128)(2,1)}), bf16[4,64,2048]{2,1,0:T(8,128)(2,1)}, u32[]{:S(2)}, u32[]{:S(2)}) async-start(bf16[4,64,2048]{2,1,0:T(8,128)(2,1)} %shard_map.141.refs_7_), calls=%async_computation.1 | async-start | bytes 2097152 | tf_op jit(solution)/shard_map/all_to_all | solution.py:510
  215.7 15.4 %collective-permute-start.27 = (bf16[4,128,2048]{2,1,0:T(8,128)(2,1)S(1)}, bf16[4,128,2048]{2,1,0:T(8,128)(2,1)}, u32[]{:S(2)}, u32[]{:S(2)}) collective-permute-start(bf16[4,128,2048]{2,1,0:T(8,128)(2,1)S(1)} %all-to-all-done.3.mine), channel_id=1, source_target_pairs={{0,1},{1,0},{2,3},{3,2},{4,5},{5,4},{6,7},{7,6},{8,9},{9,8},{10,11... | collective-permute-start | bytes 6291464 | tf_op jit(solution)/shard_map/ppermute | solution.py:507
  223.2 31.0 %all-to-all-start.2 = ((bf16[4,64,2048]{2,1,0:T(8,128)(2,1)}), bf16[4,64,2048]{2,1,0:T(8,128)(2,1)}, u32[]{:S(2)}, u32[]{:S(2)}) async-start(bf16[4,64,2048]{2,1,0:T(8,128)(2,1)} %shard_map.148.refs_10_), calls=%async_computation.2 | async-start | bytes 2097152 | tf_op jit(solution)/shard_map/all_to_all | solution.py:510
  257.4 4.8 %collective-permute-start.28 = (f32[128,128]{1,0:T(8,128)S(1)}, f32[128,128]{1,0:T(8,128)S(1)}, u32[]{:S(2)}, u32[]{:S(2)}) collective-permute-start(f32[128,128]{1,0:T(8,128)S(1)} %constant_dynamic-update-slice_fusion), channel_id=1, source_target_pairs={{0,8},{8,0},{16,24},{24,16},{1,9},{9,1},{17,25},{25,17},{2,10},{10... | collective-permute-start | bytes 196616 | tf_op jit(solution)/shard_map/ppermute | solution.py:518
  257.9 4.8 %collective-permute-start.29 = (f32[128,128]{1,0:T(8,128)S(1)}, f32[128,128]{1,0:T(8,128)S(1)}, u32[]{:S(2)}, u32[]{:S(2)}) collective-permute-start(f32[128,128]{1,0:T(8,128)S(1)} %constant_dynamic-update-slice_fusion), channel_id=1, source_target_pairs={{0,16},{8,24},{16,0},{24,8},{1,17},{9,25},{17,1},{25,9},{2,18},{10... | collective-permute-start | bytes 196616 | tf_op jit(solution)/shard_map/ppermute | solution.py:518
  258.9 5.2 %collective-permute-start.30 = (f32[128,128]{1,0:T(8,128)S(1)}, f32[128,128]{1,0:T(8,128)S(1)}, u32[]{:S(2)}, u32[]{:S(2)}) collective-permute-start(f32[128,128]{1,0:T(8,128)S(1)} %constant_dynamic-update-slice_fusion), channel_id=1, source_target_pairs={{0,24},{8,16},{16,8},{24,0},{1,25},{9,17},{17,9},{25,1},{2,26},{10... | collective-permute-start | bytes 196616 | tf_op jit(solution)/shard_map/ppermute | solution.py:518
  (32 other events, 255.5 us)

commit v3 on v2

--- a/solution.py
+++ b/solution.py
@@ -611,7 +611,8 @@
             where, mine = along, z_exchange(take(grad_out, k, sub, nz, [other]))
             mine = hold(mine, [hids[-1]])
             other = swap(mine)
-            late = [normed] if k == 1 else []
+            passed = to_pass(hid_near[-1], [normed] if k == 1 else [])
+            late = [a for two in passed.values() for a in two]
         cot, *partial = back(where, mine, other, w_down, [] if k else [note], late)
         cots.append(cot)
         parts = [partial[0]] + [row_step(partial[j], j) for j in range(1, n_row)]
@@ -621,7 +622,7 @@
             all_weights = every.transpose(2, 0, 1, 3).reshape(CHUNKS * n_row, 2 * sub, 1)
             late = []
         else:
-            late = [multiply(k - 1, to_pass(hid_near[-1], [partial[0]]), pairs[-1:])]
+            late = [multiply(k - 1, passed, pairs[-1:])]
         hids.append(hidden_grads(k, parts, gate, up, keep, weights, late))
         hid_near.append(near(hids[k]))
         if k == 0:

time: 268 us -> 266 us (level)
  transfers between devices with their start and end apart: 35 -> 35, of which waited for: 21 -> 19; matrix products, arithmetic and copies ran while one was open for 3% -> 3% of each run, Pallas kernels for 41% -> 41%
where the time goes in v3:
time: 266 us; the launch traced here: 265 us
  Pallas kernels  126 us (47%)
  waiting for transfers between devices  71.6 us (27%)
  starting transfers between devices  47.5 us (18%)
  local copies, waits for them, and re-layouts  15.2 us (6%)
  other arithmetic  3.44 us (1%)
    ppermute x23, waiting for transfers between devices, row_step(): return lax.ppermute(a, 'row', [(i, i ^ j) for i in range(n_row)])  55.7 us
    pallas_call x2, Pallas kernels, hidden(): pl.pallas_call(functools.partial(hidden_kernel, n, plan, len(slots)), out...  28.2 us
    ppermute x23, starting transfers between devices, row_step(): return lax.ppermute(a, 'row', [(i, i ^ j) for i in range(n_row)])  25.9 us
    pallas_call x1, Pallas kernels, weight_grads(): pl.pallas_call(functools.partial(weight_grads_kernel, n, plan, len(slots)...  22.6 us
    pallas_call x2, Pallas kernels, back(): pl.pallas_call(functools.partial(back_kernel, n), out_shape=(jax.ShapeDty...  19.3 us
    all_to_all x4, starting transfers between devices, z_exchange(): lax.all_to_all(a, 'col', split_axis=0, concat_axis=0, axis_index_groups=z...  17.7 us
    pallas_call x1, Pallas kernels, down_grad(): pl.pallas_call(functools.partial(down_grad_kernel, plan, len(drops)), out...  16.8 us
    ppermute x3, waiting for transfers between devices, z_next(): lax.ppermute(a, 'col', [(i, 2 * after_of[i // 2] + i % 2) for i in range(...  9.52 us
  transfers between devices with their start and end apart: 35, of which 19 were waited for; matrix products, arithmetic and copies ran while one was open for 3% of the time, Pallas kernels for 41%

profile of v3, /device:TPU:0, one launch (start us, length us, event | category | flops | bytes accessed | tf_op | source)
XLA Modules:
  0.0 264.9 jit_solution(3993763231689350799)
XLA Ops:
  0.6 3.0 %shard_map.129 = (bf16[128,1792]{1,0:T(8,128)(2,1)}, bf16[128,1792]{1,0:T(8,128)(2,1)}) custom-call(bf16[2,2,64,1792]{3,2,1,0:T(8,128)(2,1)} %bitcast.31, bf16[2,2,64,1792]{3,2,1,0:T(8,128)(2,1)} %bitcast.34, s32[2,2,64,1792]{3,2,1,0:T(8,128)} %bitcast.28), custom_call_target="tpu_custom_call" | custom-call | flops 573440 | bytes 573440 | tf_op jit(solution)/shard_map/pallas_call | solution.py:327
  3.7 2.9 %collective-permute-start.3 = (bf16[128,1792]{1,0:T(8,128)(2,1)}, bf16[128,1792]{1,0:T(8,128)(2,1)S(1)}, u32[]{:S(2)}, u32[]{:S(2)}) collective-permute-start(bf16[128,1792]{1,0:T(8,128)(2,1)} %get-tuple-element.26.refs_0_), channel_id=1, source_target_pairs={{0,8},{8,0},{16,24},{24,16},{1,9},{9,1},{17,25},{25,17},{2,10},{10... | collective-permute-start | bytes 1376264 | tf_op jit(solution)/shard_map/ppermute | solution.py:518
  11.4 7.0 %collective-permute-done.refs_1_ = bf16[64,2048]{1,0:T(8,128)(2,1)S(1)} collective-permute-done((bf16[64,2048]{1,0:T(8,128)(2,1)}, bf16[64,2048]{1,0:T(8,128)(2,1)S(1)}, u32[]{:S(2)}, u32[]{:S(2)}) %collective-permute-start) | collective-permute-done | bytes 262176 | tf_op jit(solution)/shard_map/ppermute | solution.py:515
  23.4 2.5 collective-permute-done.1.refs_2_
  26.7 6.3 %collective-permute-done.4.refs_5_.refs_2_ = bf16[128,1792]{1,0:T(8,128)(2,1)S(1)} collective-permute-done((bf16[128,1792]{1,0:T(8,128)(2,1)}, bf16[128,1792]{1,0:T(8,128)(2,1)S(1)}, u32[]{:S(2)}, u32[]{:S(2)}) %collective-permute-start.4) | collective-permute-done | bytes 458784 | tf_op jit(solution)/shard_map/ppermute | solution.py:518
  33.5 6.4 %collective-permute-done.7.refs_8_.refs_3_ = bf16[128,1792]{1,0:T(8,128)(2,1)S(1)} collective-permute-done((bf16[128,1792]{1,0:T(8,128)(2,1)S(1)}, bf16[128,1792]{1,0:T(8,128)(2,1)S(1)}, u32[]{:S(2)}, u32[]{:S(2)}) %collective-permute-start.7) | collective-permute-done | bytes 458784 | tf_op jit(solution)/shard_map/ppermute | solution.py:518
  41.4 2.2 shard_map.131.mine
  47.5 9.7 %shard_map.132 = (bf16[4,2,64,2048]{3,2,1,0:T(8,128)(2,1)}, bf16[144,1792]{1,0:T(8,128)(2,1)}, bf16[144,1792]{1,0:T(8,128)(2,1)}, bf16[144,1792]{1,0:T(8,128)(2,1)}, bf16[144,1792]{1,0:T(8,128)(2,1)}) custom-call(s32[5]{0:T(128)} %stack.81.where, bf16[4,64,2048]{2,1,0:T(8,128)(2,1)} %shard_map.131.mine, bf16[4,64,2048]{2,1,0:T(8,128)(2,1)} %copy-done.7, ...), custom_call_target="tpu_custom_call" | custom-call | flops 469762048 | bytes 1671168 | tf_op jit(solution)/shard_map/pallas_call | solution.py:287
  63.5 4.5 %all-to-all-start.1 = ((bf16[4,64,2048]{2,1,0:T(8,128)(2,1)}), bf16[4,64,2048]{2,1,0:T(8,128)(2,1)S(1)}, u32[]{:S(2)}, u32[]{:S(2)}) async-start(bf16[4,64,2048]{2,1,0:T(8,128)(2,1)} %shard_map.140), calls=%async_computation.1 | async-start | bytes 2097152 | tf_op jit(solution)/shard_map/all_to_all | solution.py:510
  68.0 4.9 %collective-permute-done.12.refs_3_ = bf16[144,1792]{1,0:T(8,128)(2,1)S(1)} collective-permute-done((bf16[144,1792]{1,0:T(8,128)(2,1)}, bf16[144,1792]{1,0:T(8,128)(2,1)S(1)}, u32[]{:S(2)}, u32[]{:S(2)}) %collective-permute-start.12) | collective-permute-done | bytes 516128 | tf_op jit(solution)/shard_map/ppermute | solution.py:518
  73.0 10.0 %collective-permute-done.11.refs_2_ = bf16[144,1792]{1,0:T(8,128)(2,1)S(1)} collective-permute-done((bf16[144,1792]{1,0:T(8,128)(2,1)}, bf16[144,1792]{1,0:T(8,128)(2,1)S(1)}, u32[]{:S(2)}, u32[]{:S(2)}) %collective-permute-start.11) | collective-permute-done | bytes 516128 | tf_op jit(solution)/shard_map/ppermute | solution.py:518
  85.1 3.8 %shard_map.133.refs_0_ = bf16[2,128,1792]{2,1,0:T(8,128)(2,1)} custom-call(bf16[144,1792]{1,0:T(8,128)(2,1)} %get-tuple-element.28.refs_0_, bf16[144,1792]{1,0:T(8,128)(2,1)} %copy-done.21, bf16[144,1792]{1,0:T(8,128)(2,1)} %copy-done.20, bf16[144,1792]{1,0:T(8,128)(2,1)} %copy-done.19, bf16[2,2,64,1792]{3,2,1,0:T(8,128)(2,1)} %bitcast.32, ...), custom_call_target="tpu_custom_call" | custom-call | flops 573440 | bytes 573440 | tf_op jit(solution)/shard_map/pallas_call | solution.py:363
  88.9 2.6 shard_map.134.refs_0_
  94.2 3.8 %all-to-all-start.3 = ((bf16[4,128,2048]{2,1,0:T(8,128)(2,1)}), bf16[4,128,2048]{2,1,0:T(8,128)(2,1)S(1)}, u32[]{:S(2)}, u32[]{:S(2)}) async-start(bf16[4,128,2048]{2,1,0:T(8,128)(2,1)} %shard_map.134.refs_0_), calls=%async_computation.3 | async-start | bytes 4194304 | tf_op jit(solution)/shard_map/all_to_all | solution.py:510
  99.6 2.3 shard_map.141.mine
  101.9 17.6 %collective-permute-done.14.a_ref.refs_2_ = bf16[2,128,1792]{2,1,0:T(8,128)(2,1)} collective-permute-done((bf16[2,128,1792]{2,1,0:T(8,128)(2,1)S(1)}, bf16[2,128,1792]{2,1,0:T(8,128)(2,1)}, u32[]{:S(2)}, u32[]{:S(2)}) %collective-permute-start.14) | collective-permute-done | bytes 917536 | tf_op jit(solution)/shard_map/ppermute | solution.py:518
  125.3 9.7 %shard_map.142 = (bf16[4,2,64,2048]{3,2,1,0:T(8,128)(2,1)}, bf16[128,1792]{1,0:T(8,128)(2,1)}, bf16[128,1792]{1,0:T(8,128)(2,1)}, bf16[128,1792]{1,0:T(8,128)(2,1)}, bf16[128,1792]{1,0:T(8,128)(2,1)}) custom-call(s32[5]{0:T(128)} %stack.97.where, bf16[4,64,2048]{2,1,0:T(8,128)(2,1)} %shard_map.141.mine, bf16[4,64,2048]{2,1,0:T(8,128)(2,1)} %collective-permute-done.18.other, ...), custom_call_target="tpu_custom_call" | custom-call | flops 469762048 | bytes 1671168 | tf_op jit(solution)/shard_map/pallas_call | solution.py:287
  140.1 14.1 %shard_map.137 = (bf16[4,64,2048]{2,1,0:T(8,128)(2,1)}, f32[4,64,2048]{2,1,0:T(8,128)}) custom-call(s32[5]{0:T(128)} %stack.97.where, bf16[2,128,1792]{2,1,0:T(8,128)(2,1)} %shard_map.133.refs_0_, bf16[2,128,1792]{2,1,0:T(8,128)(2,1)} %collective-permute-done.13.a_ref.refs_1_, bf16[2,128,1792]{2,1,0:T(8,128)(2,1)} %collective-permute-done.14.a_ref.refs_2_, ...), custom_call_target="tpu_custom_call" | custom-call | flops 939524096 | bytes 2686976 | tf_op jit(solution)/shard_map/pallas_call | solution.py:411
  157.1 3.7 %shard_map.143.refs_10_.refs_0_.refs_5_ = bf16[2,128,1792]{2,1,0:T(8,128)(2,1)} custom-call(bf16[128,1792]{1,0:T(8,128)(2,1)} %get-tuple-element.35.refs_0_, bf16[128,1792]{1,0:T(8,128)(2,1)} %copy-done.23, bf16[128,1792]{1,0:T(8,128)(2,1)} %copy-done.24, bf16[128,1792]{1,0:T(8,128)(2,1)} %collective-permute-done.21.refs_3_, ...), custom_call_target="tpu_custom_call" | custom-call | flops 573440 | bytes 573440 | tf_op jit(solution)/shard_map/pallas_call | solution.py:363
  163.3 16.8 %shard_map.144.refs_0_ = bf16[1792,2048]{1,0:T(8,128)(2,1)} custom-call(f32[8,128,1]{2,1,0:T(8,128)} %reshape.67.weight_ref, bf16[128,1792]{1,0:T(8,128)(2,1)} %get-tuple-element.26.refs_0_, bf16[128,1792]{1,0:T(8,128)(2,1)} %copy-done.8, bf16[128,1792]{1,0:T(8,128)(2,1)} %copy-done.10, bf16[128,1792]{1,0:T(8,128)(2,1)} %copy-done.12, ...), custom_call_target="tpu_custom_call" | custom-call | flops 939524096 | bytes 1900544 | tf_op jit(solution)/shard_map/pallas_call | solution.py:462
  189.0 3.0 %shard_map.138.refs_7_ = bf16[4,64,2048]{2,1,0:T(8,128)(2,1)} custom-call(f32[4,64,2048]{2,1,0:T(8,128)} %get-tuple-element.32.rest_ref, bf16[4,64,2048]{2,1,0:T(8,128)(2,1)} %collective-permute-done.17.got_ref), custom_call_target="tpu_custom_call" | custom-call | flops 65536 | bytes 524288 | tf_op jit(solution)/shard_map/pallas_call | solution.py:165
  192.0 4.5 %all-to-all-start = ((bf16[4,64,2048]{2,1,0:T(8,128)(2,1)}), bf16[4,64,2048]{2,1,0:T(8,128)(2,1)}, u32[]{:S(2)}, u32[]{:S(2)}) async-start(bf16[4,64,2048]{2,1,0:T(8,128)(2,1)} %shard_map.138.refs_7_), calls=%async_computation | async-start | bytes 2097152 | tf_op jit(solution)/shard_map/all_to_all | solution.py:510
  196.5 3.1 %collective-permute-done.24.refs_3_.refs_8_ = bf16[128,1792]{1,0:T(8,128)(2,1)S(1)} collective-permute-done((bf16[128,1792]{1,0:T(8,128)(2,1)}, bf16[128,1792]{1,0:T(8,128)(2,1)S(1)}, u32[]{:S(2)}, u32[]{:S(2)}) %collective-permute-start.24) | collective-permute-done | bytes 458784 | tf_op jit(solution)/shard_map/ppermute | solution.py:518
  200.4 14.0 %shard_map.147 = (bf16[4,64,2048]{2,1,0:T(8,128)(2,1)}, f32[4,64,2048]{2,1,0:T(8,128)}) custom-call(s32[5]{0:T(128)} %stack.97.where, bf16[2,128,1792]{2,1,0:T(8,128)(2,1)} %shard_map.143.refs_10_.refs_0_.refs_5_, bf16[2,128,1792]{2,1,0:T(8,128)(2,1)} %collective-permute-done.22.a_ref.refs_1_.refs_6_, bf16[2,128,1792]{2,1,0:T(8,128)(2,1)} %copy-done.4, ...), custom_call_target="tpu_custom_call" | custom-call | flops 939524096 | bytes 2686976 | tf_op jit(solution)/shard_map/pallas_call | solution.py:411
  215.1 3.0 %collective-permute-done.26.got_ref = bf16[4,64,2048]{2,1,0:T(8,128)(2,1)S(1)} collective-permute-done((bf16[4,64,2048]{2,1,0:T(8,128)(2,1)}, bf16[4,64,2048]{2,1,0:T(8,128)(2,1)S(1)}, u32[]{:S(2)}, u32[]{:S(2)}) %collective-permute-start.26) | collective-permute-done | bytes 1048608 | tf_op jit(solution)/shard_map/ppermute | solution.py:507
  219.0 3.0 %shard_map.148.refs_10_ = bf16[4,64,2048]{2,1,0:T(8,128)(2,1)} custom-call(f32[4,64,2048]{2,1,0:T(8,128)} %get-tuple-element.41.rest_ref, bf16[4,64,2048]{2,1,0:T(8,128)(2,1)} %copy-done.18), custom_call_target="tpu_custom_call" | custom-call | flops 65536 | bytes 524288 | tf_op jit(solution)/shard_map/pallas_call | solution.py:165
  222.0 4.8 %all-to-all-start.2 = ((bf16[4,64,2048]{2,1,0:T(8,128)(2,1)}), bf16[4,64,2048]{2,1,0:T(8,128)(2,1)}, u32[]{:S(2)}, u32[]{:S(2)}) async-start(bf16[4,64,2048]{2,1,0:T(8,128)(2,1)} %shard_map.148.refs_10_), calls=%async_computation.2 | async-start | bytes 2097152 | tf_op jit(solution)/shard_map/all_to_all | solution.py:510
  226.9 2.3 shard_map.139
  229.9 22.6 %shard_map.149 = (bf16[2048,1792]{1,0:T(8,128)(2,1)}, bf16[2048,1792]{1,0:T(8,128)(2,1)}) custom-call(s32[5]{0:T(128)} %stack.97.where, bf16[4,128,2048]{2,1,0:T(8,128)(2,1)} %copy-done.3, bf16[4,128,2048]{2,1,0:T(8,128)(2,1)} %collective-permute-done.27.other, bf16[2,128,1792]{2,1,0:T(8,128)(2,1)} %shard_map.133.refs_0_, ...), custom_call_target="tpu_custom_call" | custom-call | flops 1879048192 | bytes 3276800 | tf_op jit(solution)/shard_map/pallas_call | solution.py:245
  253.0 2.4 shard_map.150
  257.5 2.2 collective-permute-start.30
  262.8 2.2 fusion.4
  (154 shorter events, 62.9 us)
Async XLA Ops:
  3.7 16.7 %collective-permute-start.3 = (bf16[128,1792]{1,0:T(8,128)(2,1)}, bf16[128,1792]{1,0:T(8,128)(2,1)S(1)}, u32[]{:S(2)}, u32[]{:S(2)}) collective-permute-start(bf16[128,1792]{1,0:T(8,128)(2,1)} %get-tuple-element.26.refs_0_), channel_id=1, source_target_pairs={{0,8},{8,0},{16,24},{24,16},{1,9},{9,1},{17,25},{25,17},{2,10},{10... | collective-permute-start | bytes 1376264 | tf_op jit(solution)/shard_map/ppermute | solution.py:518
  6.6 15.3 %collective-permute-start.6 = (bf16[128,1792]{1,0:T(8,128)(2,1)}, bf16[128,1792]{1,0:T(8,128)(2,1)S(1)}, u32[]{:S(2)}, u32[]{:S(2)}) collective-permute-start(bf16[128,1792]{1,0:T(8,128)(2,1)} %get-tuple-element.27.refs_4_), channel_id=1, source_target_pairs={{0,16},{8,24},{16,0},{24,8},{1,17},{9,25},{17,1},{25,9},{2,18},{10... | collective-permute-start | bytes 1376264 | tf_op jit(solution)/shard_map/ppermute | solution.py:518
  9.8 8.6 %collective-permute-start = (bf16[64,2048]{1,0:T(8,128)(2,1)}, bf16[64,2048]{1,0:T(8,128)(2,1)S(1)}, u32[]{:S(2)}, u32[]{:S(2)}) collective-permute-start(bf16[64,2048]{1,0:T(8,128)(2,1)} %bitcast.37), channel_id=1, source_target_pairs={{0,2},{1,3},{2,6},{3,7},{4,0},{5,1},{6,4},{7,5},{8,10},{9,11},{10,... | collective-permute-start | bytes 786440 | tf_op jit(solution)/shard_map/ppermute | solution.py:515
  18.4 7.5 %collective-permute-start.1 = (bf16[64,2048]{1,0:T(8,128)(2,1)S(1)}, bf16[64,2048]{1,0:T(8,128)(2,1)S(1)}, u32[]{:S(2)}, u32[]{:S(2)}) collective-permute-start(bf16[64,2048]{1,0:T(8,128)(2,1)S(1)} %collective-permute-done.refs_1_), channel_id=1, source_target_pairs={{0,2},{1,3},{2,6},{3,7},{4,0},{5,1},{6,4},{7,5},{8,10},{9,11},{10,... | collective-permute-start | bytes 786440 | tf_op jit(solution)/shard_map/ppermute | solution.py:515
  19.3 13.7 %collective-permute-start.4 = (bf16[128,1792]{1,0:T(8,128)(2,1)}, bf16[128,1792]{1,0:T(8,128)(2,1)S(1)}, u32[]{:S(2)}, u32[]{:S(2)}) collective-permute-start(bf16[128,1792]{1,0:T(8,128)(2,1)} %get-tuple-element.26.refs_0_), channel_id=1, source_target_pairs={{0,16},{8,24},{16,0},{24,8},{1,17},{9,25},{17,1},{25,9},{2,18},{10... | collective-permute-start | bytes 1376264 | tf_op jit(solution)/shard_map/ppermute | solution.py:518
  19.8 13.7 %collective-permute-start.5 = (bf16[128,1792]{1,0:T(8,128)(2,1)}, bf16[128,1792]{1,0:T(8,128)(2,1)S(1)}, u32[]{:S(2)}, u32[]{:S(2)}) collective-permute-start(bf16[128,1792]{1,0:T(8,128)(2,1)} %get-tuple-element.27.refs_4_), channel_id=1, source_target_pairs={{0,8},{8,0},{16,24},{24,16},{1,9},{9,1},{17,25},{25,17},{2,10},{10... | collective-permute-start | bytes 1376264 | tf_op jit(solution)/shard_map/ppermute | solution.py:518
  20.3 19.5 %collective-permute-start.7 = (bf16[128,1792]{1,0:T(8,128)(2,1)S(1)}, bf16[128,1792]{1,0:T(8,128)(2,1)S(1)}, u32[]{:S(2)}, u32[]{:S(2)}) collective-permute-start(bf16[128,1792]{1,0:T(8,128)(2,1)S(1)} %collective-permute-done.3.refs_4_.refs_1_), channel_id=1, source_target_pairs={{0,16},{8,24},{16,0},{24,8},{1,17},{9,25},{17,1},{25,9},{2,18},{10... | collective-permute-start | bytes 1376264 | tf_op jit(solution)/shard_map/ppermute | solution.py:518
  21.9 18.2 %collective-permute-start.8 = (bf16[128,1792]{1,0:T(8,128)(2,1)S(1)}, bf16[128,1792]{1,0:T(8,128)(2,1)S(1)}, u32[]{:S(2)}, u32[]{:S(2)}) collective-permute-start(bf16[128,1792]{1,0:T(8,128)(2,1)S(1)} %collective-permute-done.6.refs_7_.refs_6_), channel_id=1, source_target_pairs={{0,8},{8,0},{16,24},{24,16},{1,9},{9,1},{17,25},{25,17},{2,10},{10... | collective-permute-start | bytes 1376264 | tf_op jit(solution)/shard_map/ppermute | solution.py:518
  25.9 7.6 %collective-permute-start.2 = (bf16[64,2048]{1,0:T(8,128)(2,1)S(1)}, bf16[64,2048]{1,0:T(8,128)(2,1)S(1)}, u32[]{:S(2)}, u32[]{:S(2)}) collective-permute-start(bf16[64,2048]{1,0:T(8,128)(2,1)S(1)} %collective-permute-done.1.refs_2_), channel_id=1, source_target_pairs={{0,2},{1,3},{2,6},{3,7},{4,0},{5,1},{6,4},{7,5},{8,10},{9,11},{10,... | collective-permute-start | bytes 786440 | tf_op jit(solution)/shard_map/ppermute | solution.py:515
  57.2 15.8 %collective-permute-start.12 = (bf16[144,1792]{1,0:T(8,128)(2,1)}, bf16[144,1792]{1,0:T(8,128)(2,1)S(1)}, u32[]{:S(2)}, u32[]{:S(2)}) collective-permute-start(bf16[144,1792]{1,0:T(8,128)(2,1)} %get-tuple-element.31), channel_id=1, source_target_pairs={{0,24},{8,16},{16,8},{24,0},{1,25},{9,17},{17,9},{25,1},{2,26},{10... | collective-permute-start | bytes 1548296 | tf_op jit(solution)/shard_map/ppermute | solution.py:518
  58.2 24.8 %collective-permute-start.11 = (bf16[144,1792]{1,0:T(8,128)(2,1)}, bf16[144,1792]{1,0:T(8,128)(2,1)S(1)}, u32[]{:S(2)}, u32[]{:S(2)}) collective-permute-start(bf16[144,1792]{1,0:T(8,128)(2,1)} %get-tuple-element.30), channel_id=1, source_target_pairs={{0,16},{8,24},{16,0},{24,8},{1,17},{9,25},{17,1},{25,9},{2,18},{10... | collective-permute-start | bytes 1548296 | tf_op jit(solution)/shard_map/ppermute | solution.py:518
  59.2 23.8 %collective-permute-start.10 = (bf16[144,1792]{1,0:T(8,128)(2,1)}, bf16[144,1792]{1,0:T(8,128)(2,1)S(1)}, u32[]{:S(2)}, u32[]{:S(2)}) collective-permute-start(bf16[144,1792]{1,0:T(8,128)(2,1)} %get-tuple-element.29), channel_id=1, source_target_pairs={{0,8},{8,0},{16,24},{24,16},{1,9},{9,1},{17,25},{25,17},{2,10},{10... | collective-permute-start | bytes 1548296 | tf_op jit(solution)/shard_map/ppermute | solution.py:518
  63.5 29.7 %all-to-all-start.1 = ((bf16[4,64,2048]{2,1,0:T(8,128)(2,1)}), bf16[4,64,2048]{2,1,0:T(8,128)(2,1)S(1)}, u32[]{:S(2)}, u32[]{:S(2)}) async-start(bf16[4,64,2048]{2,1,0:T(8,128)(2,1)} %shard_map.140), calls=%async_computation.1 | async-start | bytes 2097152 | tf_op jit(solution)/shard_map/all_to_all | solution.py:510
  94.2 97.8 %all-to-all-start.3 = ((bf16[4,128,2048]{2,1,0:T(8,128)(2,1)}), bf16[4,128,2048]{2,1,0:T(8,128)(2,1)S(1)}, u32[]{:S(2)}, u32[]{:S(2)}) async-start(bf16[4,128,2048]{2,1,0:T(8,128)(2,1)} %shard_map.134.refs_0_), calls=%async_computation.3 | async-start | bytes 4194304 | tf_op jit(solution)/shard_map/all_to_all | solution.py:510
  98.0 21.5 %collective-permute-start.14 = (bf16[2,128,1792]{2,1,0:T(8,128)(2,1)S(1)}, bf16[2,128,1792]{2,1,0:T(8,128)(2,1)}, u32[]{:S(2)}, u32[]{:S(2)}) collective-permute-start(bf16[2,128,1792]{2,1,0:T(8,128)(2,1)S(1)} %copy-done), channel_id=1, source_target_pairs={{0,16},{8,24},{16,0},{24,8},{1,17},{9,25},{17,1},{25,9},{2,18},{10... | collective-permute-start | bytes 2752520 | tf_op jit(solution)/shard_map/ppermute | solution.py:518
  99.1 22.8 %collective-permute-start.13 = (bf16[2,128,1792]{2,1,0:T(8,128)(2,1)S(1)}, bf16[2,128,1792]{2,1,0:T(8,128)(2,1)}, u32[]{:S(2)}, u32[]{:S(2)}) collective-permute-start(bf16[2,128,1792]{2,1,0:T(8,128)(2,1)S(1)} %copy-done), channel_id=1, source_target_pairs={{0,8},{8,0},{16,24},{24,16},{1,9},{9,1},{17,25},{25,17},{2,10},{10... | collective-permute-start | bytes 2752520 | tf_op jit(solution)/shard_map/ppermute | solution.py:518
  101.9 23.4 %collective-permute-start.18 = (bf16[4,64,2048]{2,1,0:T(8,128)(2,1)}, bf16[4,64,2048]{2,1,0:T(8,128)(2,1)}, u32[]{:S(2)}, u32[]{:S(2)}) collective-permute-start(bf16[4,64,2048]{2,1,0:T(8,128)(2,1)} %shard_map.141.mine), channel_id=1, source_target_pairs={{0,1},{1,0},{2,3},{3,2},{4,5},{5,4},{6,7},{7,6},{8,9},{9,8},{10,11... | collective-permute-start | bytes 3145736 | tf_op jit(solution)/shard_map/ppermute | solution.py:507
  121.3 17.2 %collective-permute-start.16 = (bf16[128,1792]{1,0:T(8,128)(2,1)}, bf16[128,1792]{1,0:T(8,128)(2,1)S(1)}, u32[]{:S(2)}, u32[]{:S(2)}) collective-permute-start(bf16[128,1792]{1,0:T(8,128)(2,1)} %shard_map.136.refs_1_), channel_id=1, source_target_pairs={{0,8},{8,0},{16,24},{24,16},{1,9},{9,1},{17,25},{25,17},{2,10},{10... | collective-permute-start | bytes 1376264 | tf_op jit(solution)/shard_map/ppermute | solution.py:518
  123.7 14.9 %collective-permute-start.15 = (bf16[128,1792]{1,0:T(8,128)(2,1)}, bf16[128,1792]{1,0:T(8,128)(2,1)S(1)}, u32[]{:S(2)}, u32[]{:S(2)}) collective-permute-start(bf16[128,1792]{1,0:T(8,128)(2,1)} %shard_map.135.refs_0_), channel_id=1, source_target_pairs={{0,16},{8,24},{16,0},{24,8},{1,17},{9,25},{17,1},{25,9},{2,18},{10... | collective-permute-start | bytes 1376264 | tf_op jit(solution)/shard_map/ppermute | solution.py:518
  135.0 19.3 %collective-permute-start.19 = (bf16[128,1792]{1,0:T(8,128)(2,1)}, bf16[128,1792]{1,0:T(8,128)(2,1)S(1)}, u32[]{:S(2)}, u32[]{:S(2)}) collective-permute-start(bf16[128,1792]{1,0:T(8,128)(2,1)} %get-tuple-element.36), channel_id=1, source_target_pairs={{0,8},{8,0},{16,24},{24,16},{1,9},{9,1},{17,25},{25,17},{2,10},{10... | collective-permute-start | bytes 1376264 | tf_op jit(solution)/shard_map/ppermute | solution.py:518
  136.5 19.8 %collective-permute-start.20 = (bf16[128,1792]{1,0:T(8,128)(2,1)}, bf16[128,1792]{1,0:T(8,128)(2,1)S(1)}, u32[]{:S(2)}, u32[]{:S(2)}) collective-permute-start(bf16[128,1792]{1,0:T(8,128)(2,1)} %get-tuple-element.37), channel_id=1, source_target_pairs={{0,16},{8,24},{16,0},{24,8},{1,17},{9,25},{17,1},{25,9},{2,18},{10... | collective-permute-start | bytes 1376264 | tf_op jit(solution)/shard_map/ppermute | solution.py:518
  137.5 18.7 %collective-permute-start.21 = (bf16[128,1792]{1,0:T(8,128)(2,1)}, bf16[128,1792]{1,0:T(8,128)(2,1)}, u32[]{:S(2)}, u32[]{:S(2)}) collective-permute-start(bf16[128,1792]{1,0:T(8,128)(2,1)} %get-tuple-element.38), channel_id=1, source_target_pairs={{0,24},{8,16},{16,8},{24,0},{1,25},{9,17},{17,9},{25,1},{2,26},{10... | collective-permute-start | bytes 1376264 | tf_op jit(solution)/shard_map/ppermute | solution.py:518
  154.2 34.8 %collective-permute-start.17 = (bf16[4,64,2048]{2,1,0:T(8,128)(2,1)}, bf16[4,64,2048]{2,1,0:T(8,128)(2,1)}, u32[]{:S(2)}, u32[]{:S(2)}) collective-permute-start(bf16[4,64,2048]{2,1,0:T(8,128)(2,1)} %get-tuple-element.33.refs_8_), channel_id=1, source_target_pairs={{0,1},{1,0},{2,3},{3,2},{4,5},{5,4},{6,7},{7,6},{8,9},{9,8},{10,11... | collective-permute-start | bytes 3145736 | tf_op jit(solution)/shard_map/ppermute | solution.py:507
  160.8 21.1 %collective-permute-start.23 = (bf16[2,128,1792]{2,1,0:T(8,128)(2,1)}, bf16[2,128,1792]{2,1,0:T(8,128)(2,1)S(1)}, u32[]{:S(2)}, u32[]{:S(2)}) collective-permute-start(bf16[2,128,1792]{2,1,0:T(8,128)(2,1)} %shard_map.143.refs_10_.refs_0_.refs_5_), channel_id=1, source_target_pairs={{0,16},{8,24},{16,0},{24,8},{1,17},{9,25},{17,1},{25,9},{2,18},{10... | collective-permute-start | bytes 2752520 | tf_op jit(solution)/shard_map/ppermute | solution.py:518
  161.8 24.3 %collective-permute-start.22 = (bf16[2,128,1792]{2,1,0:T(8,128)(2,1)}, bf16[2,128,1792]{2,1,0:T(8,128)(2,1)}, u32[]{:S(2)}, u32[]{:S(2)}) collective-permute-start(bf16[2,128,1792]{2,1,0:T(8,128)(2,1)} %shard_map.143.refs_10_.refs_0_.refs_5_), channel_id=1, source_target_pairs={{0,8},{8,0},{16,24},{24,16},{1,9},{9,1},{17,25},{25,17},{2,10},{10... | collective-permute-start | bytes 2752520 | tf_op jit(solution)/shard_map/ppermute | solution.py:518
  184.7 11.9 %collective-permute-start.25 = (bf16[128,1792]{1,0:T(8,128)(2,1)}, bf16[128,1792]{1,0:T(8,128)(2,1)S(1)}, u32[]{:S(2)}, u32[]{:S(2)}) collective-permute-start(bf16[128,1792]{1,0:T(8,128)(2,1)} %shard_map.146), channel_id=1, source_target_pairs={{0,8},{8,0},{16,24},{24,16},{1,9},{9,1},{17,25},{25,17},{2,10},{10... | collective-permute-start | bytes 1376264 | tf_op jit(solution)/shard_map/ppermute | solution.py:518
  188.0 11.7 %collective-permute-start.24 = (bf16[128,1792]{1,0:T(8,128)(2,1)}, bf16[128,1792]{1,0:T(8,128)(2,1)S(1)}, u32[]{:S(2)}, u32[]{:S(2)}) collective-permute-start(bf16[128,1792]{1,0:T(8,128)(2,1)} %shard_map.145), channel_id=1, source_target_pairs={{0,16},{8,24},{16,0},{24,8},{1,17},{9,25},{17,1},{25,9},{2,18},{10... | collective-permute-start | bytes 1376264 | tf_op jit(solution)/shard_map/ppermute | solution.py:518
  192.0 30.0 %all-to-all-start = ((bf16[4,64,2048]{2,1,0:T(8,128)(2,1)}), bf16[4,64,2048]{2,1,0:T(8,128)(2,1)}, u32[]{:S(2)}, u32[]{:S(2)}) async-start(bf16[4,64,2048]{2,1,0:T(8,128)(2,1)} %shard_map.138.refs_7_), calls=%async_computation | async-start | bytes 2097152 | tf_op jit(solution)/shard_map/all_to_all | solution.py:510
  214.6 15.3 %collective-permute-start.27 = (bf16[4,128,2048]{2,1,0:T(8,128)(2,1)S(1)}, bf16[4,128,2048]{2,1,0:T(8,128)(2,1)}, u32[]{:S(2)}, u32[]{:S(2)}) collective-permute-start(bf16[4,128,2048]{2,1,0:T(8,128)(2,1)S(1)} %all-to-all-done.3.mine), channel_id=1, source_target_pairs={{0,1},{1,0},{2,3},{3,2},{4,5},{5,4},{6,7},{7,6},{8,9},{9,8},{10,11... | collective-permute-start | bytes 6291464 | tf_op jit(solution)/shard_map/ppermute | solution.py:507
  222.0 31.0 %all-to-all-start.2 = ((bf16[4,64,2048]{2,1,0:T(8,128)(2,1)}), bf16[4,64,2048]{2,1,0:T(8,128)(2,1)}, u32[]{:S(2)}, u32[]{:S(2)}) async-start(bf16[4,64,2048]{2,1,0:T(8,128)(2,1)} %shard_map.148.refs_10_), calls=%async_computation.2 | async-start | bytes 2097152 | tf_op jit(solution)/shard_map/all_to_all | solution.py:510
  256.5 4.8 %collective-permute-start.29 = (f32[128,128]{1,0:T(8,128)S(1)}, f32[128,128]{1,0:T(8,128)S(1)}, u32[]{:S(2)}, u32[]{:S(2)}) collective-permute-start(f32[128,128]{1,0:T(8,128)S(1)} %constant_dynamic-update-slice_fusion), channel_id=1, source_target_pairs={{0,16},{8,24},{16,0},{24,8},{1,17},{9,25},{17,1},{25,9},{2,18},{10... | collective-permute-start | bytes 196616 | tf_op jit(solution)/shard_map/ppermute | solution.py:518
  257.5 5.2 %collective-permute-start.30 = (f32[128,128]{1,0:T(8,128)S(1)}, f32[128,128]{1,0:T(8,128)S(1)}, u32[]{:S(2)}, u32[]{:S(2)}) collective-permute-start(f32[128,128]{1,0:T(8,128)S(1)} %constant_dynamic-update-slice_fusion), channel_id=1, source_target_pairs={{0,24},{8,16},{16,8},{24,0},{1,25},{9,17},{17,9},{25,1},{2,26},{10... | collective-permute-start | bytes 196616 | tf_op jit(solution)/shard_map/ppermute | solution.py:518
  (32 other events, 261.4 us)
